TPU v7x, 32 devices: a whole 2x2x4 slice. The times are simulated.
32 devices in a mesh: head: 2 (over y), blk: 16 (over z, x, core).
Axes of the slice: x: 2, y: 2, z: 4, core: 2. Of those that a mesh axis runs over, the one named last changes fastest.
Arguments:
- tokens: bfloat16 [4096, 1536], P(('head', 'blk')), may hold values from -6 to 6
- cotangent: bfloat16 [4096, 1536], P(('head', 'blk')), may hold values from -6 to 6
- seq_lengths: int32 [3], replicated, may hold values from 1 to 2048, 4096 in all
- piece_order: int32 [32], replicated, may hold values from 0 to 31, each once
- routes: int32 [4096, 6], P(('head', 'blk')), may hold values from 0 to 15, all different within a row; in each aligned block of 128 rows (0 to 127, 128 to 255, ...) at most 64 rows name the same one
- norm1_gain: bfloat16 [1536], P(('head', 'blk')), may hold values from 0.5 to 1.5
- w_query: bfloat16 [1536, 1536], P(('head', 'blk')), may hold values from -0.15625 to 0.15625
- w_key: bfloat16 [1536, 512], P(('head', 'blk')), may hold values from -0.15625 to 0.15625
- w_value: bfloat16 [1536, 512], P(('head', 'blk')), may hold values from -0.15625 to 0.15625
- w_out: bfloat16 [1536, 1536], P(('head', 'blk')), may hold values from -1.75 to 1.75
- norm2_gain: bfloat16 [1536], P(('head', 'blk')), may hold values from 0.5 to 1.5
- w_router: bfloat16 [1536, 16], P(('head', 'blk')), may hold values from -0.078125 to 0.078125
- shared_up: bfloat16 [1536, 2048], P(('head', 'blk')), may hold values from -0.15625 to 0.15625
- shared_down: bfloat16 [1024, 1536], P(('head', 'blk')), may hold values from -0.1875 to 0.1875
- expert_up: bfloat16 [16, 1536, 1024], P('blk', 'head'), may hold values from -0.15625 to 0.15625
- expert_down: bfloat16 [16, 512, 1536], P('blk', None, 'head'), may hold values from -0.25 to 0.25
Outputs:
- output: bfloat16 [4096, 1536], P(('head', 'blk'))
- input_grad: float32 [4096, 1536], P(('head', 'blk'))
- norm1_gain_grad: float32 [1536], P(('head', 'blk'))
- w_query_grad: float32 [1536, 1536], P(('head', 'blk'))
- w_key_grad: float32 [1536, 512], P(('head', 'blk'))
- w_value_grad: float32 [1536, 512], P(('head', 'blk'))
- w_out_grad: float32 [1536, 1536], P(('head', 'blk'))
- norm2_gain_grad: float32 [1536], P(('head', 'blk'))
- w_router_grad: float32 [1536, 16], P(('head', 'blk'))
- shared_up_grad: float32 [1536, 2048], P(('head', 'blk'))
- shared_down_grad: float32 [1024, 1536], P(('head', 'blk'))
- expert_up_grad: float32 [16, 1536, 1024], P('blk', 'head')
- expert_down_grad: float32 [16, 512, 1536], P('blk', None, 'head')
Inputs may be any that keep to these rules, and one draw needn't show every extreme that they name: `routes`: every row names 6 different experts. Among the 128 rows of one device no expert is named more than 64 times; in every draw some device names some expert exactly 64 times. `seq_lengths`: the lengths sum to 4096; the largest is exactly 2048. Each number appears once: dealt piece p holds the stream positions piece_order[p] * 128 to piece_order[p] * 128 + 127.
All inputs are finite; a program needn't handle non-finite values.
Results may differ from a plain program's by a relative error of at most 0.025.
Values may be sent and summed in bfloat16 or wider, within the bound.
A program may use at most 256 MiB of HBM per device.

v0:
```python
import math

import jax
import jax.numpy as jnp
from jax import lax
from jax.sharding import PartitionSpec as P

H = 12
KVH = 4
HD = 128
TOP = 6
PIECE = 128


epsilon = 1e-05
neg_big = -1e30


def for_sending(array):
    return jax.tree.map(lambda a: a.astype(jnp.bfloat16) if a.dtype == jnp.float32 else a, array)


def dot_first(former, latter):
    return lax.dot_general(
        former, latter, (((0,), (0,)), ((), ())), preferred_element_type=jnp.float32
    )


def dot_last(former, latter):
    return lax.dot_general(
        former, latter, (((1,), (1,)), ((), ())), preferred_element_type=jnp.float32
    )


def inv_scale(values):
    return lax.rsqrt(jnp.mean(values * values, axis=1) + epsilon)


def norm_back(values, scaler, norm_gain, upstream):
    normed = values * scaler[:, None]
    gain_grad = jnp.sum(upstream * normed, axis=0)
    scaled_up = upstream * norm_gain
    values_grad = scaler[:, None] * (
        scaled_up - normed * jnp.mean(scaled_up * normed, axis=1, keepdims=True)
    )
    return (values_grad, gain_grad)


def locate(cycle_index, layout):
    shard_rows, blk_count, head_count, piece_order, seq_ends = layout
    owner_blk = cycle_index // (head_count * shard_rows)
    within = cycle_index % (head_count * shard_rows)
    dealt_row = (
        within // shard_rows * (blk_count * shard_rows)
        + owner_blk * shard_rows
        + within % shard_rows
    )
    piece_index = dealt_row // PIECE
    piece_ids = jnp.arange(piece_order.shape[0], dtype=jnp.int32)
    placed = jnp.sum(
        jnp.where(piece_index[:, None] == piece_ids[None, :], piece_order[None, :], 0), axis=1
    )
    position = placed * PIECE + dealt_row % PIECE
    member = jnp.sum((seq_ends[None, :] <= position[:, None]).astype(jnp.int32), axis=1)
    return (position, member)


def visible(query_where, key_where):
    query_pos, query_seq = query_where
    key_pos, key_seq = key_where
    allowed = (query_seq[:, None] == key_seq[None, :]) & (key_pos[None, :] <= query_pos[:, None])
    return allowed[:, None, None, :]


def score_block(query_heads, key_part):
    key_heads = key_part.reshape(key_part.shape[0], query_heads.shape[1], query_heads.shape[3])
    raw_scores = jnp.einsum(
        "qgrh,kgh->qgrk", query_heads, key_heads, preferred_element_type=jnp.float32
    )
    return raw_scores * query_heads.shape[3] ** (-0.5)


def pair_grads(
    query_heads, grad_heads, log_total, delta_sum, query_where, key_part, value_part, key_where
):
    allowed = visible(query_where, key_where)
    weights = jnp.where(
        allowed, jnp.exp(score_block(query_heads, key_part) - log_total[..., None]), 0.0
    )
    value_heads = value_part.reshape(
        value_part.shape[0], query_heads.shape[1], query_heads.shape[3]
    )
    prob_grad = jnp.einsum(
        "qgrh,kgh->qgrk", grad_heads, value_heads, preferred_element_type=jnp.float32
    )
    score_grad = (weights * (prob_grad - delta_sum[..., None])).astype(jnp.bfloat16)
    return (weights, score_grad)


def by_blocks(step_fn, folded, pieces):
    rows_total = pieces[0].shape[0]
    block_rows = math.gcd(rows_total, 2048)
    blocks = rows_total // block_rows
    stacked = tuple(
        (array_in.reshape((blocks, block_rows) + array_in.shape[1:]) for array_in in pieces)
    )

    def advance(running, scan_item):
        number, part_set = scan_item
        return (step_fn(running, part_set, number * block_rows), None)

    folded, unused = lax.scan(advance, folded, (jnp.arange(blocks, dtype=jnp.int32), stacked))
    return folded


def to_heads(arrays):
    return jax.tree.map(
        lambda part, own: part.astype(own.dtype),
        lax.all_to_all(for_sending(arrays), "head", split_axis=1, concat_axis=0, tiled=True),
        arrays,
    )


def from_heads(arrays):
    return jax.tree.map(
        lambda part, own: part.astype(own.dtype),
        lax.all_to_all(for_sending(arrays), "head", split_axis=0, concat_axis=1, tiled=True),
        arrays,
    )


def to_experts(rows_flat, experts, capacity):
    shaped = rows_flat.reshape(experts, capacity, rows_flat.shape[1])
    moved = lax.all_to_all(shaped, "blk", split_axis=0, concat_axis=0, tiled=True)
    return moved.reshape(experts * capacity, rows_flat.shape[1])


def from_experts(rows_flat, experts, capacity):
    shaped = rows_flat.reshape(experts, capacity, rows_flat.shape[1])
    moved = lax.all_to_all(shaped, "blk", split_axis=0, concat_axis=0, tiled=True)
    return moved.reshape(experts * capacity, rows_flat.shape[1])


def gated_grad(act_grad, gate_part, up_part):
    sigmoid_gate = jax.nn.sigmoid(gate_part)
    gate_grad = act_grad * up_part * sigmoid_gate * (1.0 + gate_part * (1.0 - sigmoid_gate))
    up_grad = act_grad * gate_part * sigmoid_gate
    return jnp.concatenate([gate_grad, up_grad], axis=1).astype(jnp.bfloat16)


def shards(
    tokens,
    cotangent,
    seq_lengths,
    piece_order,
    routes,
    norm1_gain,
    w_query,
    w_key,
    w_value,
    w_out,
    norm2_gain,
    w_router,
    shared_up,
    shared_down,
    expert_up,
    expert_down,
):
    head_count = lax.axis_size("head")
    blk_count = lax.axis_size("blk")
    dense_set = (
        lax.all_gather(w_query, ("head", "blk"), axis=0, tiled=True),
        lax.all_gather(w_key, ("head", "blk"), axis=0, tiled=True),
        lax.all_gather(w_value, ("head", "blk"), axis=0, tiled=True),
        lax.all_gather(w_out, ("head", "blk"), axis=0, tiled=True),
        lax.all_gather(w_router, ("head", "blk"), axis=0, tiled=True),
        lax.all_gather(shared_up, ("head", "blk"), axis=0, tiled=True),
        lax.all_gather(shared_down, ("head", "blk"), axis=0, tiled=True),
        lax.all_gather(norm1_gain, ("head", "blk"), axis=0, tiled=True),
        lax.all_gather(norm2_gain, ("head", "blk"), axis=0, tiled=True),
    )
    (
        full_query,
        full_key,
        full_value,
        full_out,
        full_router,
        full_up,
        full_down,
        gain_one,
        gain_two,
    ) = dense_set
    up_whole, down_whole = (
        lax.all_gather(expert_up, "head", axis=1, tiled=True),
        lax.all_gather(expert_down, "head", axis=2, tiled=True),
    )
    expert_in = up_whole[0]
    expert_out = down_whole[0]
    shard_rows = tokens.shape[0]
    groups = KVH // head_count
    repeats = H // KVH
    head_dim = HD
    score_scale = head_dim ** (-0.5)
    gain_first = gain_one.astype(jnp.float32)
    gain_second = gain_two.astype(jnp.float32)
    inputs = tokens.astype(jnp.float32)
    scaler_one = inv_scale(inputs)
    normed_one = (inputs * scaler_one[:, None] * gain_first).astype(jnp.bfloat16)
    query_rows = jnp.dot(normed_one, full_query, preferred_element_type=jnp.float32).astype(
        jnp.bfloat16
    )
    key_rows = jnp.dot(normed_one, full_key, preferred_element_type=jnp.float32).astype(
        jnp.bfloat16
    )
    value_rows = jnp.dot(normed_one, full_value, preferred_element_type=jnp.float32).astype(
        jnp.bfloat16
    )
    query_local, key_local, value_local = to_heads((query_rows, key_rows, value_rows))
    local_rows = query_local.shape[0]
    seq_ends = jnp.cumsum(seq_lengths)
    layout = (shard_rows, blk_count, head_count, piece_order, seq_ends)
    own_where = locate(
        lax.axis_index("blk") * local_rows + jnp.arange(local_rows, dtype=jnp.int32), layout
    )
    query_heads = query_local.reshape(local_rows, groups, repeats, head_dim)

    def forward_block(folded, pieces, first_row):
        running_max, running_sum, running_acc = folded
        key_part, value_part = pieces
        part_rows = key_part.shape[0]
        allowed = visible(
            own_where, locate(first_row + jnp.arange(part_rows, dtype=jnp.int32), layout)
        )
        masked = jnp.where(allowed, score_block(query_heads, key_part), neg_big)
        new_max = jnp.maximum(running_max, jnp.max(masked, axis=-1))
        weights = jnp.where(allowed, jnp.exp(masked - new_max[..., None]), 0.0)
        factor = jnp.exp(running_max - new_max)
        value_heads = value_part.reshape(part_rows, groups, head_dim)
        update = jnp.einsum(
            "qgrk,kgh->qgrh",
            weights.astype(jnp.bfloat16),
            value_heads,
            preferred_element_type=jnp.float32,
        )
        return (
            new_max,
            running_sum * factor + jnp.sum(weights, axis=-1),
            running_acc * factor[..., None] + update,
        )

    stats_shape = (local_rows, groups, repeats)
    start_state = (
        jnp.full(stats_shape, neg_big, jnp.float32),
        jnp.zeros(stats_shape, jnp.float32),
        jnp.zeros(stats_shape + (head_dim,), jnp.float32),
    )
    final_max, final_sum, final_acc = by_blocks(
        forward_block,
        start_state,
        (
            lax.all_gather(key_local, "blk", axis=0, tiled=True),
            lax.all_gather(value_local, "blk", axis=0, tiled=True),
        ),
    )
    attended = final_acc / final_sum[..., None]
    log_total = final_max + jnp.log(final_sum)
    mixed_out = from_heads(
        (attended.reshape(local_rows, repeats * groups * head_dim).astype(jnp.bfloat16),)
    )[0]
    hidden_res = inputs + jnp.dot(mixed_out, full_out, preferred_element_type=jnp.float32)
    scaler_two = inv_scale(hidden_res)
    normed_two = (hidden_res * scaler_two[:, None] * gain_second).astype(jnp.bfloat16)
    capacity = shard_rows * TOP * 4 // (3 * blk_count)
    logits = jnp.dot(normed_two, full_router, preferred_element_type=jnp.float32)
    route_hot = routes[:, :, None] == jnp.arange(blk_count, dtype=jnp.int32)[None, None, :]
    chosen = jnp.sum(jnp.where(route_hot, logits[:, None, :], 0.0), axis=2)
    gate_probs = jax.nn.softmax(chosen, axis=1)
    flat_hot = route_hot.reshape(shard_rows * TOP, blk_count).astype(jnp.int32)
    earlier = jnp.sum((jnp.cumsum(flat_hot, axis=0) - flat_hot) * flat_hot, axis=1)
    slot_ids = routes.reshape(shard_rows * TOP) * capacity + earlier
    slot_hot = (
        slot_ids[:, None] == jnp.arange(blk_count * capacity, dtype=jnp.int32)[None, :]
    ).astype(jnp.bfloat16)
    token_hot = jnp.sum(slot_hot.reshape(shard_rows, TOP, blk_count * capacity), axis=1)
    dispatched = dot_first(token_hot, normed_two).astype(jnp.bfloat16)
    expert_rows = to_experts(dispatched, blk_count, capacity)
    both_parts = jnp.dot(expert_rows, expert_in, preferred_element_type=jnp.float32)
    expert_width = expert_out.shape[0]
    gate_part = both_parts[:, :expert_width]
    up_part = both_parts[:, expert_width:]
    activated = (jax.nn.silu(gate_part) * up_part).astype(jnp.bfloat16)
    expert_result = jnp.dot(activated, expert_out, preferred_element_type=jnp.float32).astype(
        jnp.bfloat16
    )
    returned = from_experts(expert_result, blk_count, capacity)
    picked = jnp.take(returned, slot_ids, axis=0).reshape(shard_rows, TOP, returned.shape[1])
    routed_sum = jnp.sum(gate_probs[:, :, None] * picked.astype(jnp.float32), axis=1)
    shared_both = jnp.dot(normed_two, full_up, preferred_element_type=jnp.float32)
    shared_width = full_down.shape[0]
    shared_gate = shared_both[:, :shared_width]
    shared_lift = shared_both[:, shared_width:]
    shared_act = (jax.nn.silu(shared_gate) * shared_lift).astype(jnp.bfloat16)
    shared_sum = jnp.dot(shared_act, full_down, preferred_element_type=jnp.float32)
    output = (hidden_res + routed_sum + shared_sum).astype(jnp.bfloat16)
    grad_out = cotangent.astype(jnp.float32)
    gate_grad = jnp.einsum("tkd,td->tk", picked, cotangent, preferred_element_type=jnp.float32)
    slot_grad = (
        (gate_probs[:, :, None] * grad_out[:, None, :])
        .astype(jnp.bfloat16)
        .reshape(shard_rows * TOP, grad_out.shape[1])
    )
    slot_rows = dot_first(slot_hot, slot_grad).astype(jnp.bfloat16)
    expert_grad_rows = to_experts(slot_rows, blk_count, capacity)
    act_grad = dot_last(expert_grad_rows, expert_out)
    grad_down = dot_first(activated, expert_grad_rows)
    both_grad = gated_grad(act_grad, gate_part, up_part)
    grad_in = dot_first(expert_rows, both_grad)
    rows_back = dot_last(both_grad, expert_in).astype(jnp.bfloat16)
    rows_home = from_experts(rows_back, blk_count, capacity)
    norm_two_grad = jnp.dot(token_hot, rows_home, preferred_element_type=jnp.float32)
    expert_up_grad, expert_down_grad = (
        lax.psum_scatter(
            grad_in[None].astype(jnp.bfloat16), "head", scatter_dimension=1, tiled=True
        ).astype(jnp.float32),
        lax.psum_scatter(
            grad_down[None].astype(jnp.bfloat16), "head", scatter_dimension=2, tiled=True
        ).astype(jnp.float32),
    )
    weighted = gate_probs * gate_grad
    chosen_grad = weighted - gate_probs * jnp.sum(weighted, axis=1, keepdims=True)
    logit_grad = jnp.sum(jnp.where(route_hot, chosen_grad[:, :, None], 0.0), axis=1).astype(
        jnp.bfloat16
    )
    router_grad = dot_first(normed_two, logit_grad)
    norm_two_grad = norm_two_grad + dot_last(logit_grad, full_router)
    shared_down_grad = dot_first(shared_act, cotangent)
    shared_act_grad = dot_last(cotangent, full_down)
    shared_both_grad = gated_grad(shared_act_grad, shared_gate, shared_lift)
    shared_up_grad = dot_first(normed_two, shared_both_grad)
    norm_two_grad = norm_two_grad + dot_last(shared_both_grad, full_up)
    residual_grad, gain_two_grad = norm_back(hidden_res, scaler_two, gain_second, norm_two_grad)
    hidden_grad = grad_out + residual_grad
    hidden_low = hidden_grad.astype(jnp.bfloat16)
    out_grad = dot_first(mixed_out, hidden_low)
    mixed_grad = dot_last(hidden_low, full_out).astype(jnp.bfloat16)
    grad_local = to_heads((mixed_grad,))[0]
    grad_heads = grad_local.reshape(local_rows, groups, repeats, head_dim)
    delta_sum = jnp.sum(grad_heads.astype(jnp.float32) * attended, axis=-1)
    query_zero = jnp.zeros(stats_shape + (head_dim,), jnp.float32)

    def key_block(folded, pieces, first_row):
        query_grad, key_value_grad = folded
        key_part, value_part = pieces
        part_rows = key_part.shape[0]
        key_where = locate(first_row + jnp.arange(part_rows, dtype=jnp.int32), layout)
        weights, score_grad = pair_grads(
            query_heads,
            grad_heads,
            log_total,
            delta_sum,
            own_where,
            key_part,
            value_part,
            key_where,
        )
        key_heads = key_part.reshape(part_rows, groups, head_dim)
        query_grad = query_grad + score_scale * jnp.einsum(
            "qgrk,kgh->qgrh", score_grad, key_heads, preferred_element_type=jnp.float32
        )
        key_part_grad = score_scale * jnp.einsum(
            "qgrk,qgrh->kgh", score_grad, query_heads, preferred_element_type=jnp.float32
        )
        value_part_grad = jnp.einsum(
            "qgrk,qgrh->kgh",
            weights.astype(jnp.bfloat16),
            grad_heads,
            preferred_element_type=jnp.float32,
        )
        joined = jnp.stack([key_part_grad, value_part_grad], axis=1)
        previous = lax.dynamic_slice_in_dim(key_value_grad, first_row, part_rows, 0)
        return (
            query_grad,
            lax.dynamic_update_slice_in_dim(key_value_grad, previous + joined, first_row, 0),
        )

    all_zero = jnp.zeros((blk_count * local_rows, 2, groups, head_dim), jnp.float32)
    query_grad, all_pairs = by_blocks(
        key_block,
        (query_zero, all_zero),
        (
            lax.all_gather(key_local, "blk", axis=0, tiled=True),
            lax.all_gather(value_local, "blk", axis=0, tiled=True),
        ),
    )
    own_pairs = lax.psum_scatter(all_pairs, "blk", scatter_dimension=0, tiled=True)
    key_grad = own_pairs[:, 0]
    value_grad = own_pairs[:, 1]
    query_back, key_back, value_back = from_heads(
        (
            query_grad.reshape(local_rows, groups * repeats * head_dim).astype(jnp.bfloat16),
            key_grad.reshape(local_rows, groups * head_dim).astype(jnp.bfloat16),
            value_grad.reshape(local_rows, groups * head_dim).astype(jnp.bfloat16),
        )
    )
    query_w_grad = dot_first(normed_one, query_back)
    key_w_grad = dot_first(normed_one, key_back)
    value_w_grad = dot_first(normed_one, value_back)
    norm_one_grad = (
        dot_last(query_back, full_query)
        + dot_last(key_back, full_key)
        + dot_last(value_back, full_value)
    )
    input_extra, gain_one_grad = norm_back(inputs, scaler_one, gain_first, norm_one_grad)
    input_grad = hidden_grad + input_extra
    summed = (
        lax.psum_scatter(query_w_grad, ("head", "blk"), scatter_dimension=0, tiled=True),
        lax.psum_scatter(key_w_grad, ("head", "blk"), scatter_dimension=0, tiled=True),
        lax.psum_scatter(value_w_grad, ("head", "blk"), scatter_dimension=0, tiled=True),
        lax.psum_scatter(out_grad, ("head", "blk"), scatter_dimension=0, tiled=True),
        lax.psum_scatter(router_grad, ("head", "blk"), scatter_dimension=0, tiled=True),
        lax.psum_scatter(shared_up_grad, ("head", "blk"), scatter_dimension=0, tiled=True),
        lax.psum_scatter(shared_down_grad, ("head", "blk"), scatter_dimension=0, tiled=True),
        lax.psum_scatter(gain_one_grad, ("head", "blk"), scatter_dimension=0, tiled=True),
        lax.psum_scatter(gain_two_grad, ("head", "blk"), scatter_dimension=0, tiled=True),
    )
    return (
        output,
        input_grad,
        summed[7],
        summed[0],
        summed[1],
        summed[2],
        summed[3],
        summed[8],
        summed[4],
        summed[5],
        summed[6],
        expert_up_grad,
        expert_down_grad,
    )


def solution(mesh):
    placed = (
        P(("head", "blk"), None),
        P(("head", "blk"), None),
        P(),
        P(),
        P(("head", "blk"), None),
        P(("head", "blk")),
        P(("head", "blk"), None),
        P(("head", "blk"), None),
        P(("head", "blk"), None),
        P(("head", "blk"), None),
        P(("head", "blk")),
        P(("head", "blk"), None),
        P(("head", "blk"), None),
        P(("head", "blk"), None),
        P("blk", "head", None),
        P("blk", None, "head"),
    )
    return jax.shard_map(
        shards,
        mesh=mesh,
        in_specs=placed,
        out_specs=(
            P(("head", "blk"), None),
            P(("head", "blk"), None),
            P(("head", "blk")),
            P(("head", "blk"), None),
            P(("head", "blk"), None),
            P(("head", "blk"), None),
            P(("head", "blk"), None),
            P(("head", "blk")),
            P(("head", "blk"), None),
            P(("head", "blk"), None),
            P(("head", "blk"), None),
            P("blk", "head", None),
            P("blk", None, "head"),
        ),
        check_vma=False,
    )
```

profile of v0, /device:TPU:0, one launch (start us, length us, event | category | flops | bytes accessed | tf_op | source)
XLA Modules:
  0.0 1927.3 jit_solution(12534773004787415862)
XLA Ops:
  12.0 42.2 %all-reduce.5 = (bf16[1536]{0:T(1024)(128)(2,1)S(1)}, bf16[1536]{0:T(1024)(128)(2,1)S(1)}) all-reduce(bf16[1536]{0:T(1024)(128)(2,1)S(1)} %dynamic-update-slice, bf16[1536]{0:T(1024)(128)(2,1)S(1)} %dynamic-update-slice.1), channel_id=1, replica_groups=mesh['head'=2,'blk'=16] {'head','blk'}, use_global_device_ids=true, to_apply=%add | all-reduce | flops 3072 | bytes 12288
  79.1 47.2 %all-gather.12.cloned.1.call-done = bf16[1536,512]{1,0:T(8,128)(2,1)} async-done(((bf16[48,512]{1,0:T(8,128)(2,1)}), bf16[1536,512]{1,0:T(8,128)(2,1)}) %all-gather.12.cloned.1.call-update) | async-done | bytes 1572880 | tf_op jit(solution)/shard_map/all_gather | solution.py:173
  139.1 52.6 %all-gather.16.cloned.1.call-done = bf16[1536,1536]{1,0:T(8,128)(2,1)} async-done(((bf16[48,1536]{1,0:T(8,128)(2,1)}), bf16[1536,1536]{1,0:T(8,128)(2,1)}) %all-gather.16.cloned.1.call-update) | async-done | bytes 4718608 | tf_op jit(solution)/shard_map/all_gather | solution.py:172
  200.2 33.6 %all-gather.20.cloned.1.call-done = bf16[4096,256]{1,0:T(8,128)(2,1)} async-done(((bf16[256,256]{1,0:T(8,128)(2,1)}), bf16[4096,256]{1,0:T(8,128)(2,1)}) %all-gather.20.cloned.1.call-update) | async-done | bytes 2097168 | tf_op jit(solution)/shard_map/all_gather | solution.py:262
  237.9 38.2 %all-gather.14.cloned.1.call-done = bf16[4096,256]{1,0:T(8,128)(2,1)} async-done(((bf16[256,256]{1,0:T(8,128)(2,1)}), bf16[4096,256]{1,0:T(8,128)(2,1)}) %all-gather.14.cloned.1.call-update) | async-done | bytes 2097168 | tf_op jit(solution)/shard_map/all_gather | solution.py:261
  281.7 30.1 %while.34 = (s32[]{:T(128)}, f32[256,2,3]{0,2,1:T(4,128)S(1)}, f32[256,2,3]{0,2,1:T(4,128)S(1)}, f32[256,2,3,128]{0,3,2,1:T(8,128)S(1)}, s32[256]{0:T(256)S(1)},...) while((s32[]{:T(128)}, f32[256,2,3]{0,2,1:T(4,128)S(1)}, ...), condition=%wide.region_9.10_spmd.clone, body=%wide.region_4.9_spmd.clone.sunk | while | flops 1654121984 | bytes 48277836 | solution.py:112
  317.4 23.8 %all-gather.22.cloned.1.call-done = bf16[1536,1536]{1,0:T(8,128)(2,1)} async-done(((bf16[48,1536]{1,0:T(8,128)(2,1)}), bf16[1536,1536]{1,0:T(8,128)(2,1)}) %all-gather.22.cloned.1.call-update) | async-done | bytes 4718608 | tf_op jit(solution)/shard_map/all_gather | solution.py:175
  353.9 46.3 %all-gather.24.cloned.1.call-done = bf16[1,1536,1024]{2,1,0:T(8,128)(2,1)} async-done(((bf16[1,768,1024]{2,1,0:T(8,128)(2,1)}), bf16[1,1536,1024]{2,1,0:T(8,128)(2,1)}) %all-gather.24.cloned.1.call-update) | async-done | bytes 3145744 | tf_op jit(solution)/shard_map/all_gather | solution.py:194
  449.4 110.8 %all-gather = bf16[32,48,16]{1,2,0:T(8,128)(2,1)S(1)} all-gather(bf16[1,48,16]{1,2,0:T(8,128)(2,1)} %bitcast.340), channel_id=1, replica_groups=mesh['head'=2,'blk'=16] {'head','blk'}, dimensions={0}, use_global_device_ids=true | all-gather | bytes 50688 | tf_op jit(solution)/shard_map/all_gather | solution.py:176
  607.4 64.4 %all-to-all-done.6 = bf16[16,64,1536]{2,1,0:T(8,128)(2,1)S(1)} async-done(((bf16[16,64,1536]{2,1,0:T(8,128)(2,1)}), bf16[16,64,1536]{2,1,0:T(8,128)(2,1)S(1)}, u32[]{:S(2)}, u32[]{:S(2)}) %all-to-all-start.6) | async-done | bytes 3145760 | tf_op jit(solution)/shard_map/all_to_all | solution.py:134
  683.1 16.1 all-to-all-start.7
  709.8 48.8 %all-to-all-done.7 = bf16[16,64,1536]{2,1,0:T(8,128)(2,1)} async-done(((bf16[16,64,1536]{2,1,0:T(8,128)(2,1)}), bf16[16,64,1536]{2,1,0:T(8,128)(2,1)}, u32[]{:S(2)}, u32[]{:S(2)}) %all-to-all-start.7) | async-done | bytes 3145760 | tf_op jit(solution)/shard_map/all_to_all | solution.py:140
  783.2 69.6 %while.35 = (s32[]{:T(128)}, f32[256,2,3,128]{0,3,2,1:T(8,128)}, f32[4096,2,2,128]{3,0,2,1:T(8,128)}, bf16[2,2048,256]{1,2,0:T(8,128)(2,1)}, s32[256]{0:T(256)S(...) while((s32[]{:T(128)}, f32[256,2,3,128]{0,3,2,1:T(8,128)}, ...), condition=%wide.region_26.27_spmd.clone, body=%wide.region_23.26_spmd.clone.sunk | while | flops 4063217664 | bytes 212980592 | solution.py:112
  902.9 64.0 %reduce-scatter.13.cloned.1.call-done = f32[256,2,2,128]{3,0,2,1:T(8,128)} async-done(((f32[4096,2,2,128]{3,0,2,1:T(8,128)}), f32[256,2,2,128]{3,0,2,1:T(8,128)}) %reduce-scatter.13.cloned.1.call-update) | async-done | bytes 524304 | tf_op jit(solution)/shard_map/reduce_scatter | solution.py:395
  993.9 73.1 %reduce-scatter.31.cloned.1.call-done = f32[48,16]{1,0:T(8,128)} async-done(((f32[1536,16]{1,0:T(8,128)}), f32[48,16]{1,0:T(8,128)}) %reduce-scatter.31.cloned.1.call-update) | async-done | bytes 3088
  1068.4 26.6 %reduce-scatter.29.cloned.1.call-done = bf16[1,512,768]{2,1,0:T(8,128)(2,1)} async-done(((bf16[1,512,1536]{2,1,0:T(8,128)(2,1)}), bf16[1,512,768]{2,1,0:T(8,128)(2,1)}) %reduce-scatter.29.cloned.1.call-update) | async-done | bytes 786448 | tf_op jit(solution)/shard_map/reduce_scatter | solution.py:325
  1097.4 43.2 %reduce-scatter.27.cloned.1.call-done = bf16[1,768,1024]{2,1,0:T(8,128)(2,1)} async-done(((bf16[1,1536,1024]{2,1,0:T(8,128)(2,1)}), bf16[1,768,1024]{2,1,0:T(8,128)(2,1)}) %reduce-scatter.27.cloned.1.call-update) | async-done | bytes 1572880 | tf_op jit(solution)/shard_map/reduce_scatter | solution.py:322
  1149.7 39.5 %all-reduce.4 = (f32[1536]{0:T(1024)S(1)}, f32[1536]{0:T(1024)S(1)}) all-reduce(f32[1536]{0:T(1024)S(1)} %get-tuple-element.673, f32[1536]{0:T(1024)S(1)} %copy-done.65), channel_id=3, replica_groups=mesh['head'=2,'blk'=16] {'head','blk'}, use_global_device_ids=true, to_apply=%region_30.31.clone | all-reduce | flops 3072 | bytes 24576
  1191.6 69.7 %reduce-scatter.25.cloned.1.call-done = f32[32,1536]{1,0:T(8,128)} async-done(((f32[1024,1536]{1,0:T(8,128)}), f32[32,1536]{1,0:T(8,128)}) %reduce-scatter.25.cloned.1.call-update) | async-done | bytes 196624 | tf_op jit(solution)/shard_map/reduce_scatter | solution.py:422
  1261.3 162.4 %reduce-scatter.23.cloned.1.call-done = f32[48,2048]{1,0:T(8,128)} async-done(((f32[1536,2048]{1,0:T(8,128)}), f32[48,2048]{1,0:T(8,128)}) %reduce-scatter.23.cloned.1.call-update) | async-done | bytes 393232 | tf_op jit(solution)/shard_map/reduce_scatter | solution.py:421
  1423.7 141.1 %reduce-scatter.21.cloned.1.call-done = f32[48,1536]{1,0:T(8,128)} async-done(((f32[1536,1536]{1,0:T(8,128)}), f32[48,1536]{1,0:T(8,128)}) %reduce-scatter.21.cloned.1.call-update) | async-done | bytes 294928 | tf_op jit(solution)/shard_map/reduce_scatter | solution.py:419
  1564.8 141.9 %reduce-scatter.15.cloned.1.call-done = f32[48,1536]{1,0:T(8,128)} async-done(((f32[1536,1536]{1,0:T(8,128)}), f32[48,1536]{1,0:T(8,128)}) %reduce-scatter.15.cloned.1.call-update) | async-done | bytes 294928 | tf_op jit(solution)/shard_map/reduce_scatter | solution.py:416
  1706.7 106.4 %reduce-scatter.19.cloned.1.call-done = f32[48,512]{1,0:T(8,128)} async-done(((f32[1536,512]{1,0:T(8,128)}), f32[48,512]{1,0:T(8,128)}) %reduce-scatter.19.cloned.1.call-update) | async-done | bytes 98320 | tf_op jit(solution)/shard_map/reduce_scatter | solution.py:418
  1813.1 106.3 %reduce-scatter.17.cloned.1.call-done = f32[48,512]{1,0:T(8,128)} async-done(((f32[1536,512]{1,0:T(8,128)}), f32[48,512]{1,0:T(8,128)}) %reduce-scatter.17.cloned.1.call-update) | async-done | bytes 98320 | tf_op jit(solution)/shard_map/reduce_scatter | solution.py:417
  (431 shorter events, 408.5 us)
Async XLA Ops:
  8.0 61.5 %all-gather.18.cloned.1.call-start = ((), (), s32[]{:S(2)}) async-start(), calls=%async_computation.25 | async-start | bytes 1622016 | tf_op jit(solution)/shard_map/all_gather | solution.py:174
  8.8 117.5 %all-gather.12.cloned.1.call-start = ((), (), s32[]{:S(2)}) async-start(), calls=%async_computation.22 | async-start | bytes 1622016 | tf_op jit(solution)/shard_map/all_gather | solution.py:173
  9.5 182.1 %all-gather.16.cloned.1.call-start = ((), (), s32[]{:S(2)}) async-start(), calls=%async_computation.24 | async-start | bytes 4866048 | tf_op jit(solution)/shard_map/all_gather | solution.py:172
  10.3 223.6 %all-gather.20.cloned.1.call-start = ((), (), s32[]{:S(2)}) async-start(), calls=%async_computation.26 | async-start | bytes 2228224 | tf_op jit(solution)/shard_map/all_gather | solution.py:262
  79.1 197.0 %all-gather.14.cloned.1.call-start = ((), (), s32[]{:S(2)}) async-start(), calls=%async_computation.23 | async-start | bytes 2228224 | tf_op jit(solution)/shard_map/all_gather | solution.py:261
  135.7 205.5 %all-gather.22.cloned.1.call-start = ((), (), s32[]{:S(2)}) async-start(), calls=%async_computation.27 | async-start | bytes 4866048 | tf_op jit(solution)/shard_map/all_gather | solution.py:175
  195.7 84.4 %all-to-all-start.1 = ((bf16[128,2,768]{0,2,1:T(8,128)(2,1)}), bf16[128,2,768]{0,2,1:T(8,128)(2,1)S(1)}, u32[]{:S(2)}, u32[]{:S(2)}) async-start(bf16[128,2,768]{0,2,1:T(8,128)(2,1)} %bitcast.5), calls=%async_computation.1 | async-start | bytes 786432 | tf_op jit(solution)/shard_map/all_to_all | solution.py:119
  348.3 63.8 %all-to-all-start.4 = ((bf16[16,64,1536]{2,1,0:T(8,128)(2,1)}), bf16[16,64,1536]{2,1,0:T(8,128)(2,1)S(1)}, u32[]{:S(2)}, u32[]{:S(2)}) async-start(bf16[16,64,1536]{2,1,0:T(8,128)(2,1)} %bitcast.14), calls=%async_computation.4 | async-start | bytes 6291456 | tf_op jit(solution)/shard_map/all_to_all | solution.py:134
  353.3 75.4 %all-gather.26.cloned.1.call-start = ((), (), s32[]{:S(2)}) async-start(), calls=%async_computation.29 | async-start | bytes 2359296 | tf_op jit(solution)/shard_map/all_gather | solution.py:195
  433.9 147.1 %all-to-all-start.5 = ((bf16[16,64,1536]{2,1,0:T(8,128)(2,1)}), bf16[16,64,1536]{2,1,0:T(8,128)(2,1)S(1)}, u32[]{:S(2)}, u32[]{:S(2)}) async-start(bf16[16,64,1536]{2,1,0:T(8,128)(2,1)} %bitcast.319), calls=%async_computation.5 | async-start | bytes 6291456 | tf_op jit(solution)/shard_map/all_to_all | solution.py:140
  443.0 256.2 %all-gather.28.cloned.1.call-start = ((), (), s32[]{:S(2)}) async-start(), calls=%async_computation.30 | async-start | bytes 6488064 | tf_op jit(solution)/shard_map/all_gather | solution.py:177
  602.9 68.9 %all-to-all-start.6 = ((bf16[16,64,1536]{2,1,0:T(8,128)(2,1)}), bf16[16,64,1536]{2,1,0:T(8,128)(2,1)S(1)}, u32[]{:S(2)}, u32[]{:S(2)}) async-start(bf16[16,64,1536]{2,1,0:T(8,128)(2,1)} %bitcast.320), calls=%async_computation.6 | async-start | bytes 6291456 | tf_op jit(solution)/shard_map/all_to_all | solution.py:134
  606.6 96.4 %all-gather.30.cloned.1.call-start = ((), (), s32[]{:S(2)}) async-start(), calls=%async_computation.31 | async-start | bytes 3244032 | tf_op jit(solution)/shard_map/all_gather | solution.py:178
  683.1 75.5 %all-to-all-start.7 = ((bf16[16,64,1536]{2,1,0:T(8,128)(2,1)}), bf16[16,64,1536]{2,1,0:T(8,128)(2,1)}, u32[]{:S(2)}, u32[]{:S(2)}) async-start(bf16[16,64,1536]{2,1,0:T(8,128)(2,1)} %bitcast.22), calls=%async_computation.7 | async-start | bytes 6291456 | tf_op jit(solution)/shard_map/all_to_all | solution.py:140
  769.2 197.6 %reduce-scatter.13.cloned.1.call-start = ((), (), s32[]{:S(2)}) async-start(), calls=%async_computation.32 | async-start | bytes 8912896 | tf_op jit(solution)/shard_map/reduce_scatter | solution.py:395
  852.8 214.2 %reduce-scatter.31.cloned.1.call-start = ((), (), s32[]{:S(2)}) async-start(), calls=%async_computation.41 | async-start | bytes 811008
  855.0 239.9 %reduce-scatter.29.cloned.1.call-start = ((), (), s32[]{:S(2)}) async-start(), calls=%async_computation.40 | async-start | bytes 2359296 | tf_op jit(solution)/shard_map/reduce_scatter | solution.py:325
  860.7 279.9 %reduce-scatter.27.cloned.1.call-start = ((), (), s32[]{:S(2)}) async-start(), calls=%async_computation.39 | async-start | bytes 4718592 | tf_op jit(solution)/shard_map/reduce_scatter | solution.py:322
  867.2 394.1 %reduce-scatter.25.cloned.1.call-start = ((), (), s32[]{:S(2)}) async-start(), calls=%async_computation.38 | async-start | bytes 6488064 | tf_op jit(solution)/shard_map/reduce_scatter | solution.py:422
  872.2 551.6 %reduce-scatter.23.cloned.1.call-start = ((), (), s32[]{:S(2)}) async-start(), calls=%async_computation.37 | async-start | bytes 12976128 | tf_op jit(solution)/shard_map/reduce_scatter | solution.py:421
  880.7 684.2 %reduce-scatter.21.cloned.1.call-start = ((), (), s32[]{:S(2)}) async-start(), calls=%async_computation.36 | async-start | bytes 9732096 | tf_op jit(solution)/shard_map/reduce_scatter | solution.py:419
  887.0 819.8 %reduce-scatter.15.cloned.1.call-start = ((), (), s32[]{:S(2)}) async-start(), calls=%async_computation.33 | async-start | bytes 9732096 | tf_op jit(solution)/shard_map/reduce_scatter | solution.py:416
  902.8 910.3 %reduce-scatter.19.cloned.1.call-start = ((), (), s32[]{:S(2)}) async-start(), calls=%async_computation.35 | async-start | bytes 3244032 | tf_op jit(solution)/shard_map/reduce_scatter | solution.py:418
  977.8 941.6 %reduce-scatter.17.cloned.1.call-start = ((), (), s32[]{:S(2)}) async-start(), calls=%async_computation.34 | async-start | bytes 3244032 | tf_op jit(solution)/shard_map/reduce_scatter | solution.py:417
  (98 other events, 1977.9 us)
Sparse Core Ops, SparseCore 0:
  11.7 57.7 all-gather.17
  72.4 53.8 all-gather.11
  129.1 62.4 all-gather.15
  193.7 40.1 all-gather.19
  235.9 40.1 all-gather.13
  278.8 62.3 all-gather.21
  446.8 101.5 all-gather.27
  610.4 89.3 all-gather.29
  852.9 113.8 reduce-scatter.12
  971.8 95.1 reduce-scatter.30
  1069.8 25.0 reduce-scatter.28
  1097.2 43.3 reduce-scatter.26
  1146.8 114.4 reduce-scatter.24
  1268.8 154.8 reduce-scatter.22
  1430.1 134.7 reduce-scatter.20
  1572.2 134.5 reduce-scatter.14
  1712.6 100.4 reduce-scatter.18
  1819.0 100.3 reduce-scatter.16
Sparse Core Ops, SparseCore 1:
  354.7 45.4 all-gather.23
  401.6 27.0 all-gather.25
where the time goes:
time: 1930 us
  waiting for transfers between devices  1330 us (69%)
  blocking collectives  231 us (12%)
  matrix products  164 us (8%)
  local copies, waits for them, and re-layouts  87.6 us (5%)
  starting transfers between devices  45.3 us (2%)
  other arithmetic  44.8 us (2%)
    reduce_scatter x1, waiting for transfers between devices, shards(): lax.psum_scatter(shared_up_grad, ('head', 'blk'), scatter_dimension=0, ti...  162 us
    reduce_scatter x1, waiting for transfers between devices, shards(): lax.psum_scatter(query_w_grad, ('head', 'blk'), scatter_dimension=0, tile...  142 us
    reduce_scatter x1, waiting for transfers between devices, shards(): lax.psum_scatter(out_grad, ('head', 'blk'), scatter_dimension=0, tiled=True)  141 us
    all_gather x1, blocking collectives, shards(): lax.all_gather(w_router, ('head', 'blk'), axis=0, tiled=True)  111 us
    reduce_scatter x1, waiting for transfers between devices, shards(): lax.psum_scatter(value_w_grad, ('head', 'blk'), scatter_dimension=0, tile...  106 us
    reduce_scatter x1, waiting for transfers between devices, shards(): lax.psum_scatter(key_w_grad, ('head', 'blk'), scatter_dimension=0, tiled=...  106 us
    unnamed x2, blocking collectives  81.7 us
    unnamed x21, waiting for transfers between devices  78.1 us
  transfers between devices with their start and end apart: 27, of which 22 were waited for; matrix products, arithmetic and copies ran while one was open for 10% of the time, Pallas kernels for 0%

commit v1 on v0

v1 whole, which is shorter than its diff:
```python
import functools

import jax
import jax.numpy as jnp
from jax import lax
from jax.experimental import pallas as pl
from jax.experimental.pallas import tpu as pltpu
from jax.sharding import PartitionSpec as P

MESH = pl.DeviceIdType.MESH


def ring_place(chip, chips):
    odd = chip % 2
    return (chip // 2) * (1 - odd) + (chips - 1 - chip // 2) * odd


def ring_chip(place, chips):
    high = place // (chips // 2)
    return 2 * place * (1 - high) + (2 * (chips - 1 - place) + 1) * high


def ring_info(chips):
    blk = lax.axis_index("blk")
    chip, core = blk // 2, blk % 2
    place = ring_place(chip, chips)

    def at(step):
        return ring_chip((place + step + chips) % chips, chips) * 2 + core

    return blk, core, at, blk + 1 - 2 * core


def pieces_of(shape):
    if len(shape) == 3:
        return [(0, None), (1, None)]
    rows = shape[0]
    if rows >= 32 and rows % 16 == 0:
        cut = (rows // 2 + 15) // 16 * 16
        return [(0, cut), (cut, rows - cut)]
    return [(0, rows)]


def part_in(ref, piece):
    start, size = piece
    return ref.at[start] if size is None else ref.at[pl.ds(start, size)]


def part_out(ref, piece, b):
    start, size = piece
    return ref.at[start, b] if size is None else ref.at[b, pl.ds(start, size)]


def ag_kernel(count, chips, plans, *refs):
    ins, outs = refs[:count], refs[count : 2 * count]
    right_sem, left_sem, sib_sem, sright, sleft, ssib, own_sem = refs[2 * count :]
    blk, core, at, sib = ring_info(chips)
    right, left = at(1), at(-1)
    barrier = pltpu.get_barrier_semaphore()
    for other in (right, left, sib):
        pl.semaphore_signal(barrier, inc=1, device_id={"blk": other}, device_id_type=MESH)
    pl.semaphore_wait(barrier, 3)
    half = chips // 2
    started = []

    def send(src, dst, ssem, rsem, dev):
        copy = pltpu.make_async_remote_copy(
            src_ref=src, dst_ref=dst, send_sem=ssem, recv_sem=rsem,
            device_id={"blk": dev}, device_id_type=MESH)
        copy.start()
        started.append(copy)
        return copy

    chunks = []
    for k in range(count):
        for i, piece in enumerate(plans[k]):
            chunks.append((len(chunks), k, piece, half - (i % 2), half - 1 + (i % 2)))
    copies = {}
    locals_ = []
    for c, k, piece, rh, lh in chunks:
        src = part_in(ins[k], piece)
        dst = part_out(outs[k], piece, blk)
        if rh >= 1:
            copies[c, "r", 1] = send(src, dst, sright.at[c, 0], right_sem.at[c, 0], right)
        if lh >= 1:
            copies[c, "l", 1] = send(src, dst, sleft.at[c, 0], left_sem.at[c, 0], left)
        copies[c, "s", 0] = send(src, dst, ssib.at[c, 0], sib_sem.at[c, 0], sib)
        own = pltpu.make_async_copy(src, dst, own_sem.at[c])
        own.start()
        locals_.append(own)
    for s in range(1, half + 1):
        for c, k, piece, rh, lh in chunks:
            if s <= rh:
                copies[c, "r", s].wait_recv()
                b = at(-s)
                blockref = part_out(outs[k], piece, b)
                if s < rh:
                    copies[c, "r", s + 1] = send(blockref, blockref, sright.at[c, s], right_sem.at[c, s], right)
                copies[c, "sr", s] = send(blockref, blockref, ssib.at[c, s], sib_sem.at[c, s], sib)
            if s <= lh:
                copies[c, "l", s].wait_recv()
                b = at(s)
                blockref = part_out(outs[k], piece, b)
                if s < lh:
                    copies[c, "l", s + 1] = send(blockref, blockref, sleft.at[c, s], left_sem.at[c, s], left)
                copies[c, "sl", s] = send(blockref, blockref, ssib.at[c, half + s], sib_sem.at[c, half + s], sib)
    for (c, d, s), copy in copies.items():
        if d in ("s", "sr", "sl"):
            copy.wait_recv()
    for copy in started:
        copy.wait_send()
    for copy in locals_:
        copy.wait()


def all_gather_blk(arrays, blks, collective_id, vmem=False):
    chips = blks // 2
    count = len(arrays)
    plans = [pieces_of(a.shape) for a in arrays]
    n = sum(len(p) for p in plans)
    half = chips // 2
    shapes = [
        jax.ShapeDtypeStruct((a.shape[0], blks) + a.shape[1:] if a.ndim == 3 else (blks,) + a.shape, a.dtype)
        for a in arrays
    ]
    dma = pltpu.SemaphoreType.DMA
    space = pltpu.VMEM if vmem else pl.ANY
    return pl.pallas_call(
        functools.partial(ag_kernel, count, chips, plans),
        out_shape=shapes,
        in_specs=[pl.BlockSpec(memory_space=space)] * count,
        out_specs=[pl.BlockSpec(memory_space=space)] * count,
        scratch_shapes=[
            dma((n, half)), dma((n, half)), dma((n, 2 * half + 1)),
            dma((n, half)), dma((n, half)), dma((n, 2 * half + 1)), dma((n,)),
        ],
        compiler_params=pltpu.CompilerParams(collective_id=collective_id, has_side_effects=True,
            vmem_limit_bytes=(60 << 20) if vmem else None),
    )(*arrays)


def rs_kernel(count, chips, plans, *refs):
    xs, outs = refs[:count], refs[count : 2 * count]
    rest = refs[2 * count :]
    n = sum(len(p) for p in plans)
    ys, rs, ls = rest[:n], rest[n : 2 * n], rest[2 * n : 3 * n]
    right_sem, left_sem, sib_sem, sright, sleft, ssib = rest[3 * n :]
    blk, core, at, sib = ring_info(chips)
    right, left = at(1), at(-1)
    barrier = pltpu.get_barrier_semaphore()
    for other in (right, left, sib):
        pl.semaphore_signal(barrier, inc=1, device_id={"blk": other}, device_id_type=MESH)
    pl.semaphore_wait(barrier, 3)
    half = chips // 2
    started = []

    def send(src, dst, ssem, rsem, dev):
        copy = pltpu.make_async_remote_copy(
            src_ref=src, dst_ref=dst, send_sem=ssem, recv_sem=rsem,
            device_id={"blk": dev}, device_id_type=MESH)
        copy.start()
        started.append(copy)
        return copy

    chunks = []
    for k in range(count):
        for i, piece in enumerate(plans[k]):
            chunks.append((len(chunks), k, piece, half - (i % 2), half - 1 + (i % 2)))
    order = []
    for d in range(half, 0, -1):
        order += [d, -d] if d < half else [d]
    order.append(0)
    sibs = {}
    for j, d in enumerate(order):
        there = at(d) + 1 - 2 * core
        for c, k, piece, rh, lh in chunks:
            sibs[c, d] = send(part_out(xs[k], piece, there), ys[c].at[j], ssib.at[c, j], sib_sem.at[c, j], sib)
    ready = set()

    def blocks(rows, body):
        step = 16 if rows % 16 == 0 else rows

        @pl.loop(0, rows // step)
        def _(i):
            body(pl.ds(pl.multiple_of(i * step, step), step))

    def mine(c, k, piece, d):
        j = order.index(d)
        if (c, d) not in ready:
            sibs[c, d].wait_recv()
            ready.add((c, d))
        return j

    copies = {}

    def join(c, k, piece, d, into, recv):
        j = mine(c, k, piece, d)
        x = part_out(xs[k], piece, at(d))
        rows = x.shape[0]

        def body(w):
            total = x[w].astype(jnp.float32) + ys[c][j, w].astype(jnp.float32)
            if recv is not None:
                total = total + recv[w].astype(jnp.float32)
            into[w] = total.astype(into.dtype)

        blocks(rows, body)

    for s in range(1, half + 1):
        for c, k, piece, rh, lh in chunks:
            for way, hops, buf, sem, ssem, dev in (
                (1, rh, rs[c], right_sem, sright, right),
                (-1, lh, ls[c], left_sem, sleft, left),
            ):
                if s > hops:
                    continue
                if s == 1:
                    j = order.index(way * hops if way * hops in order else hops)
                    join(c, k, piece, order[j], ys[c].at[j], None)
                    src = ys[c].at[j]
                else:
                    copies[c, way, s - 1].wait_recv()
                    d = way * (hops - s + 1)
                    src = buf.at[s - 2]
                    join(c, k, piece, d, src, src)
                copies[c, way, s] = send(src, buf.at[s - 1], ssem.at[c, s - 1], sem.at[c, s - 1], dev)
    for c, k, piece, rh, lh in chunks:
        if rh >= 1:
            copies[c, 1, rh].wait_recv()
        if lh >= 1:
            copies[c, -1, lh].wait_recv()
        j = mine(c, k, piece, 0)
        x = part_out(xs[k], piece, blk)
        target = part_in(outs[k], piece)

        def body(w, x=x, c=c, j=j, rh=rh, lh=lh, target=target):
            total = x[w].astype(jnp.float32) + ys[c][j, w].astype(jnp.float32)
            if rh >= 1:
                total = total + rs[c][rh - 1, w].astype(jnp.float32)
            if lh >= 1:
                total = total + ls[c][lh - 1, w].astype(jnp.float32)
            target[w] = total.astype(target.dtype)

        blocks(x.shape[0], body)
    for copy in started:
        copy.wait_send()


def reduce_scatter_blk(arrays, blks, collective_id, out_dtypes):
    chips = blks // 2
    half = chips // 2
    count = len(arrays)
    shapes = [a.shape[1:] if a.ndim == 3 else (2,) + a.shape[2:] for a in arrays]
    plans = [pieces_of(s) for s in shapes]
    dma = pltpu.SemaphoreType.DMA
    ys, rs = [], []
    for s, plan in zip(shapes, plans):
        for start, size in plan:
            rows = s[1] if size is None else size
            ys.append(pltpu.VMEM((chips, rows, s[-1]), jnp.bfloat16))
            rs.append(pltpu.VMEM((half, rows, s[-1]), jnp.bfloat16))
    n = len(ys)
    return pl.pallas_call(
        functools.partial(rs_kernel, count, chips, plans),
        out_shape=[jax.ShapeDtypeStruct(s, t) for s, t in zip(shapes, out_dtypes)],
        in_specs=[pl.BlockSpec(memory_space=pltpu.VMEM)] * count,
        out_specs=[pl.BlockSpec(memory_space=pltpu.VMEM)] * count,
        scratch_shapes=ys + rs + rs + [
            dma((n, half)), dma((n, half)), dma((n, chips)),
            dma((n, half)), dma((n, half)), dma((n, chips)),
        ],
        compiler_params=pltpu.CompilerParams(collective_id=collective_id, has_side_effects=True,
            vmem_limit_bytes=60 << 20),
    )(*arrays)


H = 12
KVH = 4
HD = 128
TOP = 6
PIECE = 128
EPS = 1e-05
NEG = -1e30
F32 = jnp.float32
BF16 = jnp.bfloat16


def dot(a, b):
    return jnp.dot(a, b, preferred_element_type=F32)


def dot_first(a, b):
    return lax.dot_general(a, b, (((0,), (0,)), ((), ())), preferred_element_type=F32)


def dot_last(a, b):
    return lax.dot_general(a, b, (((1,), (1,)), ((), ())), preferred_element_type=F32)


def inv_scale(values):
    return lax.rsqrt(jnp.mean(values * values, axis=1, keepdims=True) + EPS)


def norm_back(values, scaler, gain, upstream):
    normed = values * scaler
    gain_grad = jnp.sum(upstream * normed, axis=0)
    scaled = upstream * gain
    grad = scaler * (scaled - normed * jnp.mean(scaled * normed, axis=1, keepdims=True))
    return grad, gain_grad


def gated_grad(act_grad, gate, lift):
    sig = jax.nn.sigmoid(gate)
    return jnp.concatenate(
        [act_grad * lift * sig * (1.0 + gate * (1.0 - sig)), act_grad * gate * sig], axis=1
    ).astype(BF16)


def swap(array):
    return lax.ppermute(array, "head", [(0, 1), (1, 0)])


def key_span(places_ref, ends_ref, i):
    place = places_ref[i]
    start = jnp.int32(0)
    for e in range(ends_ref.shape[0]):
        start = jnp.where(ends_ref[e] <= place * PIECE, ends_ref[e], start)
    return start // PIECE, place


def key_chunk(slots_ref, first, pieces, *refs):
    last = slots_ref.shape[0] - 1
    slots = [slots_ref[jnp.minimum(first + k, last)] for k in range(pieces)]
    return slots, [jnp.concatenate([ref[s] for s in slots], axis=0) for ref in refs]


def stacked(ref, i, repeats):
    return jnp.concatenate(
        [ref[pl.ds(i * PIECE, PIECE), pl.ds(r * HD, HD)] for r in range(repeats)], axis=0)


def seen(ends_ref, place, first, keys, cols):
    own = place * PIECE + lax.broadcasted_iota(jnp.int32, (1, cols), 1) % PIECE
    start = jnp.zeros((1, cols), jnp.int32)
    for e in range(ends_ref.shape[0]):
        start = jnp.where(ends_ref[e] <= own, ends_ref[e], start)
    there = first * PIECE + lax.broadcasted_iota(jnp.int32, (keys, 1), 0)
    return (there <= own) & (there >= start)


CHUNK = 4


def forward_kernel(repeats, slots_ref, places_ref, ends_ref, q_ref, k_ref, v_ref, low_ref, full_ref, lse_ref):
    cols = repeats * PIECE
    for i in range(q_ref.shape[0] // PIECE):
        lo, place = key_span(places_ref, ends_ref, i)
        q = stacked(q_ref, i, repeats)

        def step(n, carry, lo=lo, place=place, q=q):
            top, total, acc = carry
            first = lo + n * CHUNK
            _, (k, v) = key_chunk(slots_ref, first, CHUNK, k_ref, v_ref)
            scores = dot_last(k, q) * HD**-0.5
            scores = jnp.where(seen(ends_ref, place, first, CHUNK * PIECE, cols), scores, NEG)
            new = jnp.maximum(top, jnp.max(scores, axis=0, keepdims=True))
            weights = jnp.exp(scores - new)
            factor = jnp.exp(top - new)
            total = total * factor + jnp.sum(weights, axis=0, keepdims=True)
            return new, total, acc * factor + dot_first(v, weights.astype(BF16))

        top, total, acc = lax.fori_loop(
            0, (place - lo) // CHUNK + 1, step,
            (jnp.full((1, cols), NEG, F32), jnp.zeros((1, cols), F32), jnp.zeros((HD, cols), F32)))
        out = jnp.swapaxes(acc / total, 0, 1)
        lse_ref[0, pl.ds(i, 1), :] = top + jnp.log(total)
        for r in range(repeats):
            part = out[r * PIECE : (r + 1) * PIECE]
            full_ref[pl.ds(i * PIECE, PIECE), pl.ds(r * HD, HD)] = part
            low_ref[pl.ds(i * PIECE, PIECE), pl.ds(r * HD, HD)] = part.astype(BF16)


def attention_forward(query, kv, where):
    rows, pieces = query.shape[0], kv.shape[0]
    groups = kv.shape[2] // (2 * HD)
    wide = query.shape[1] // groups
    repeats = wide // HD
    spec = pl.BlockSpec((rows, wide), lambda g, *_: (0, g))
    return pl.pallas_call(
        functools.partial(forward_kernel, repeats),
        grid_spec=pltpu.PrefetchScalarGridSpec(
            num_scalar_prefetch=3,
            grid=(groups,),
            in_specs=[
                spec,
                pl.BlockSpec((pieces, PIECE, HD), lambda g, *_: (0, 0, g)),
                pl.BlockSpec((pieces, PIECE, HD), lambda g, *_: (0, 0, groups + g)),
            ],
            out_specs=[spec, spec, pl.BlockSpec((1, rows // PIECE, repeats * PIECE), lambda g, *_: (g, 0, 0))],
        ),
        out_shape=[
            jax.ShapeDtypeStruct(query.shape, BF16),
            jax.ShapeDtypeStruct(query.shape, F32),
            jax.ShapeDtypeStruct((groups, rows // PIECE, repeats * PIECE), F32),
        ],
        compiler_params=pltpu.CompilerParams(vmem_limit_bytes=48 << 20),
    )(*where, query, kv, kv)


def backward_kernel(
    repeats, slots_ref, places_ref, ends_ref, q_ref, k_ref, v_ref, full_ref, grad_ref, lse_ref,
    dq_ref, dk_ref, dv_ref, key_acc, value_acc,
):
    cols = repeats * PIECE
    key_acc[...] = jnp.zeros_like(key_acc)
    value_acc[...] = jnp.zeros_like(value_acc)
    for i in range(q_ref.shape[0] // PIECE):
        lo, place = key_span(places_ref, ends_ref, i)
        q, grad = stacked(q_ref, i, repeats), stacked(grad_ref, i, repeats)
        product = grad.astype(F32) * stacked(full_ref, i, repeats)
        delta = jnp.sum(jnp.swapaxes(product, 0, 1), axis=0, keepdims=True)
        lse = lse_ref[0, pl.ds(i, 1), :]

        def step(n, dq, lo=lo, place=place, q=q, grad=grad, delta=delta, lse=lse):
            first = lo + n * CHUNK
            slots, (k, v) = key_chunk(slots_ref, first, CHUNK, k_ref, v_ref)
            scores = dot_last(k, q) * HD**-0.5
            weights = jnp.where(
                seen(ends_ref, place, first, CHUNK * PIECE, cols), jnp.exp(scores - lse), 0.0)
            back = (weights * (dot_last(v, grad) - delta)).astype(BF16)
            dk = dot(back, q)
            dv = dot(weights.astype(BF16), grad)
            for j, s in enumerate(slots):
                key_acc[s] += dk[j * PIECE : (j + 1) * PIECE]
                value_acc[s] += dv[j * PIECE : (j + 1) * PIECE]
            return dq + dot_first(k, back)

        dq = lax.fori_loop(0, (place - lo) // CHUNK + 1, step, jnp.zeros((HD, cols), F32))
        out = (jnp.swapaxes(dq, 0, 1) * HD**-0.5).astype(BF16)
        for r in range(repeats):
            dq_ref[pl.ds(i * PIECE, PIECE), pl.ds(r * HD, HD)] = out[r * PIECE : (r + 1) * PIECE]
    dk_ref[...] = (key_acc[...] * HD**-0.5).astype(BF16)
    dv_ref[...] = value_acc[...].astype(BF16)


def attention_backward(query, kv, full, lse, grad, where):
    rows, pieces = query.shape[0], kv.shape[0]
    groups = kv.shape[2] // (2 * HD)
    wide = query.shape[1] // groups
    repeats = wide // HD
    spec = pl.BlockSpec((rows, wide), lambda g, *_: (0, g))
    block = pl.BlockSpec((pieces, PIECE, HD), lambda g, *_: (0, 0, g))
    half = jax.ShapeDtypeStruct((pieces, PIECE, groups * HD), BF16)
    return pl.pallas_call(
        functools.partial(backward_kernel, repeats),
        grid_spec=pltpu.PrefetchScalarGridSpec(
            num_scalar_prefetch=3,
            grid=(groups,),
            in_specs=[
                spec, block, pl.BlockSpec((pieces, PIECE, HD), lambda g, *_: (0, 0, groups + g)), spec, spec,
                pl.BlockSpec((1, rows // PIECE, repeats * PIECE), lambda g, *_: (g, 0, 0)),
            ],
            out_specs=[spec, block, block],
            scratch_shapes=[pltpu.VMEM((pieces, PIECE, HD), F32)] * 2,
        ),
        out_shape=[jax.ShapeDtypeStruct(query.shape, BF16), half, half],
        compiler_params=pltpu.CompilerParams(vmem_limit_bytes=60 << 20),
    )(*where, query, kv, kv, full, grad, lse)


def shards(
    tokens, cotangent, seq_lengths, piece_order, routes, norm1_gain, w_query, w_key, w_value, w_out,
    norm2_gain, w_router, shared_up, shared_down, expert_up, expert_down,
):
    blks = lax.axis_size("blk")
    h, b = lax.axis_index("head"), lax.axis_index("blk")
    rows, width = tokens.shape
    experts = blks
    capacity = rows * TOP * 4 // (3 * blks)
    dense_rows = w_query.shape[0]

    def pair(own, other):
        return jnp.where(h == 0, jnp.stack([own, other]), jnp.stack([other, own]))

    def half(w, i, parts=1):
        size = w.shape[1] // (2 * parts)
        cut = lax.dynamic_slice_in_dim(w.reshape(w.shape[0], parts, 2 * size), i * size, size, 2)
        return cut.reshape(w.shape[0], parts * size)

    def pick(stacked, i):
        return lax.dynamic_index_in_dim(stacked, i, 0, keepdims=False)

    def columns(i):
        return jnp.concatenate([half(w_query, i), half(w_key, i), half(w_value, i)], axis=1)

    small = jnp.concatenate(
        [w_router, norm1_gain[:, None], norm2_gain[:, None],
         jnp.zeros((dense_rows, -(experts + 2) % 128), BF16)], axis=1)
    lanes = small.shape[1]
    first = pair(
        jnp.concatenate([columns(h), small], axis=1),
        swap(jnp.concatenate([columns(1 - h), small], axis=1)),
    )
    tokens_pair = pair(tokens, swap(tokens))
    cotangent_pair = pair(cotangent, swap(cotangent)).reshape(2 * rows, width)
    up_pair = pair(half(shared_up, h, 2), swap(half(shared_up, 1 - h, 2)))
    expert_in = pair(expert_up[0], swap(expert_up[0])).reshape(width, -1)
    other_down = swap(expert_down[0])
    expert_out = jnp.where(
        h == 0,
        jnp.concatenate([expert_down[0], other_down], axis=1),
        jnp.concatenate([other_down, expert_down[0]], axis=1),
    )
    gathered = all_gather_blk([first], blks, 0)[0].reshape(width, -1)
    qw = w_query.shape[1] // 2
    kw = w_key.shape[1] // 2
    full_qkv = gathered[:, : qw + 2 * kw]
    full_router = gathered[:, qw + 2 * kw : qw + 2 * kw + experts]
    gain_first = gathered[:, qw + 2 * kw + experts].astype(F32)
    gain_second = gathered[:, qw + 2 * kw + experts + 1].astype(F32)

    inputs_pair = tokens_pair.reshape(2 * rows, width).astype(F32)
    normed_one = (inputs_pair * inv_scale(inputs_pair) * gain_first).astype(BF16)
    qkv = dot(normed_one, full_qkv).astype(BF16)
    query = qkv[:, :qw]
    kv = all_gather_blk([qkv[:, qw:]], blks, 1)[0].reshape(-1, PIECE, 2 * kw)

    places = jnp.swapaxes(piece_order.reshape(2, blks), 0, 1).reshape(-1)
    order = jnp.arange(2 * blks, dtype=jnp.int32)
    slots = jnp.sum(jnp.where(places[None, :] == order[:, None], order[None, :], 0), axis=1)
    where = (slots, lax.dynamic_slice_in_dim(places, 2 * b, 2), jnp.cumsum(seq_lengths))
    attended, attended_full, lse = attention_forward(query, kv, where)

    up_all, out_all, down_all, cot_all = all_gather_blk([up_pair, w_out, shared_down, cotangent], blks, 2)
    full_up = up_all.reshape(width, -1)
    full_out = out_all.reshape(-1, width)
    full_down = down_all.reshape(-1, width)
    shared_width = full_down.shape[0]

    mixed = dot(attended, full_out).reshape(2, rows, width)
    inputs = tokens.astype(F32)
    resid = inputs + (pick(mixed, h) + swap(pick(mixed, 1 - h).astype(BF16)).astype(F32))
    scaler_two = inv_scale(resid)
    normed_two = (resid * scaler_two * gain_second).astype(BF16)
    normed_pair = pair(normed_two, swap(normed_two)).reshape(2 * rows, width)

    logits = dot(normed_two, full_router)
    hot = routes[:, :, None] == jnp.arange(experts, dtype=jnp.int32)[None, None, :]
    mask = jnp.any(hot, axis=1)
    masked = jnp.where(mask, logits, NEG)
    raised = jnp.where(mask, jnp.exp(masked - jnp.max(masked, axis=1, keepdims=True)), 0.0)
    gates = raised / jnp.sum(raised, axis=1, keepdims=True)
    extra = jnp.concatenate(
        [gates.astype(BF16), mask.astype(BF16), jnp.zeros((rows, -2 * experts % 128), BF16)], axis=1)

    ext = all_gather_blk([jnp.concatenate([normed_two, extra], axis=1)], blks, 3)[0]
    norm_all = ext[:, :, :width]
    gate_here = lax.dynamic_index_in_dim(ext, width + b, 2, keepdims=False).astype(F32)
    mask_here = lax.dynamic_index_in_dim(ext, width + experts + b, 2, keepdims=False).astype(F32)
    rank = jnp.cumsum(mask_here, axis=1) - mask_here
    slots = jnp.arange(capacity, dtype=F32)
    deal = ((rank[:, None, :] == slots[None, :, None]) & (mask_here[:, None, :] > 0)).astype(BF16)
    deal_gate = deal * gate_here[:, None, :].astype(BF16)

    def to_slots(dealer, array):
        moved = jnp.einsum("bst,btd->bsd", dealer, array, preferred_element_type=F32)
        return moved.astype(BF16).reshape(blks * capacity, width)

    def to_rows(dealer, array):
        return jnp.einsum(
            "bst,bsd->btd", dealer, array.reshape(blks, capacity, width), preferred_element_type=F32)

    expert_rows = to_slots(deal, norm_all)
    both = dot(expert_rows, expert_in)
    ew = expert_out.shape[0]
    gate_part, up_part = both[:, :ew], both[:, ew:]
    activated = (jax.nn.silu(gate_part) * up_part).astype(BF16)
    result = dot(activated, expert_out).astype(BF16)
    result_rows = to_rows(deal, result)
    gate_grad = jnp.sum(result_rows * cot_all.astype(F32), axis=2, keepdims=True)
    routed = (result_rows * gate_here[:, :, None]).astype(BF16)
    slot_grad = to_slots(deal_gate, cot_all)
    act_grad = dot_last(slot_grad, expert_out)
    both_grad = gated_grad(act_grad, gate_part, up_part)
    rows_back = to_rows(deal, dot_last(both_grad, expert_in).astype(BF16)).astype(BF16)
    lane = jnp.arange(128 * (-(-2 * experts // 128)), dtype=jnp.int32)
    grad_high = gate_grad.astype(BF16)
    grad_low = (gate_grad - grad_high.astype(F32)).astype(BF16)
    grad_lanes = jnp.where(lane == b, grad_high, jnp.where(lane == b + experts, grad_low, jnp.zeros((), BF16)))
    home = reduce_scatter_blk([jnp.concatenate([rows_back, grad_lanes], axis=2)], blks, 4, [F32])[0]
    routed_sum = reduce_scatter_blk([routed], blks, 5, [F32])[0]
    dwn = dot_first(activated, slot_grad)
    dup = dot_first(expert_rows, both_grad).reshape(2, width // 2, -1)
    dwn = jnp.stack([dwn[:, : width // 2], dwn[:, width // 2 :]])
    expert_up_grad = pick(dup, h) + swap(pick(dup, 1 - h).astype(BF16)).astype(F32)
    expert_down_grad = pick(dwn, h) + swap(pick(dwn, 1 - h).astype(BF16)).astype(F32)

    shared_both = dot(normed_pair, full_up)
    shared_gate, shared_lift = shared_both[:, :shared_width], shared_both[:, shared_width:]
    shared_act = (jax.nn.silu(shared_gate) * shared_lift).astype(BF16)
    shared_sum = dot(shared_act, full_down).reshape(2, rows, width)
    shared_down_part = dot_first(shared_act, cotangent_pair)
    shared_grad = gated_grad(dot_last(cotangent_pair, full_down), shared_gate, shared_lift)
    shared_up_part = dot_first(normed_pair, shared_grad)
    shared_back = dot_last(shared_grad, full_up).reshape(2, rows, width)
    output = (
        resid + routed_sum + pick(shared_sum, h) + swap(pick(shared_sum, 1 - h).astype(BF16)).astype(F32)
    ).astype(BF16)

    dgate = home[:, width : width + experts] + home[:, width + experts : width + 2 * experts]
    weighted = gates * dgate
    logit_grad = (weighted - gates * jnp.sum(weighted, axis=1, keepdims=True)).astype(BF16)
    router_part = dot_first(normed_two, logit_grad)
    norm_two_grad = (
        home[:, :width] + dot_last(logit_grad, full_router)
        + pick(shared_back, h) + swap(pick(shared_back, 1 - h).astype(BF16)).astype(F32)
    )
    back, gain_two_part = norm_back(resid, scaler_two, gain_second, norm_two_grad)
    hidden_grad = cotangent.astype(F32) + back
    hidden_low = hidden_grad.astype(BF16)
    hidden_pair = pair(hidden_low, swap(hidden_low)).reshape(2 * rows, width)
    out_part = dot_first(attended, hidden_pair)
    mixed_grad = dot_last(hidden_pair, full_out).astype(BF16)
    query_grad, *kv_parts = attention_backward(query, kv, attended_full, lse, mixed_grad, where)
    kv_grads = reduce_scatter_blk([part.reshape(blks, 2 * rows, kw) for part in kv_parts], blks, 6, [BF16] * 2)
    qkv_grad = jnp.concatenate([query_grad, *kv_grads], axis=1)
    norm_one_part = dot_last(qkv_grad, full_qkv).reshape(2, rows, width)
    norm_one_grad = pick(norm_one_part, h) + swap(pick(norm_one_part, 1 - h).astype(BF16)).astype(F32)
    extra_grad, gain_one_part = norm_back(inputs, inv_scale(inputs), gain_first, norm_one_grad)
    input_grad = hidden_grad + extra_grad
    qkv_part = dot_first(normed_one, qkv_grad)
    small_part = jnp.concatenate(
        [router_part, gain_one_part[:, None], gain_two_part[:, None],
         jnp.zeros((width, lanes - experts - 2), F32)], axis=1)

    def by_rows(part):
        return part.astype(BF16).reshape(2, blks, dense_rows, -1)

    qkv_sum, up_sum, out_sum, down_sum, small_sum = reduce_scatter_blk(
        [by_rows(qkv_part), by_rows(shared_up_part),
         out_part.astype(BF16).reshape(blks, dense_rows, width),
         shared_down_part.astype(BF16).reshape(blks, -1, width), by_rows(small_part)],
        blks, 7, [BF16, BF16, F32, F32, F32])
    there = swap(jnp.concatenate([pick(qkv_sum, 1 - h), pick(up_sum, 1 - h)], axis=1)).astype(F32)
    here = jnp.concatenate([pick(qkv_sum, h), pick(up_sum, h)], axis=1).astype(F32)
    small_sum = pick(small_sum, h) + swap(pick(small_sum, 1 - h))

    def whole(start, size):
        return jnp.where(
            h == 0,
            jnp.concatenate([here[:, start : start + size], there[:, start : start + size]], axis=1),
            jnp.concatenate([there[:, start : start + size], here[:, start : start + size]], axis=1))

    top = qw + 2 * kw
    sw = shared_width
    up_grad = jnp.concatenate([whole(top, sw), whole(top + sw, sw)], axis=1)
    return (
        output, input_grad, small_sum[:, experts], whole(0, qw), whole(qw, kw), whole(qw + kw, kw),
        out_sum, small_sum[:, experts + 1], small_sum[:, :experts], up_grad, down_sum,
        expert_up_grad[None], expert_down_grad[None],
    )


def solution(mesh):
    both = P(("head", "blk"), None)
    flat = P(("head", "blk"))
    up, down = P("blk", "head", None), P("blk", None, "head")
    return jax.shard_map(
        shards,
        mesh=mesh,
        in_specs=(both, both, P(), P(), both, flat, both, both, both, both, flat, both, both, both, up, down),
        out_specs=(both, both, flat, both, both, both, both, flat, both, both, both, up, down),
        check_vma=False,
    )
```

time: 1930 us -> 579 us (0.30)
  waiting for transfers between devices: 1330 us -> 10.6 us
  Pallas kernels: 0 us -> 375 us
  blocking collectives: 231 us -> 0 us
  matrix products: 164 us -> 62.5 us
  local copies, waits for them, and re-layouts: 87.6 us -> 56.7 us
  starting transfers between devices: 45.3 us -> 18.2 us
    reduce_scatter x9 -> x0, waiting for transfers between devices: 862 us -> none  [the longest x1 162 us: shards(): lax.psum_scatter(shared_up_grad, ('head', 'blk'), scatter_dimension=0, ti...]
    pallas_call x0 -> x10, Pallas kernels: none -> 375 us  [the longest x4 186 us: reduce_scatter_blk(): pl.pallas_call(functools.partial(rs_kernel, count, chips, plans), out_sha...]
    all_gather x10 -> x0, waiting for transfers between devices: 262 us -> none  [the longest x1 52.6 us: shards(): lax.all_gather(w_query, ('head', 'blk'), axis=0, tiled=True)]
    all_to_all x7 -> x0, waiting for transfers between devices: 132 us -> none  [the longest x2 76.3 us: to_experts(): lax.all_to_all(shaped, 'blk', split_axis=0, concat_axis=0, tiled=True)]
    all_gather x1 -> x0, blocking collectives: 111 us -> none  [shards(): lax.all_gather(w_router, ('head', 'blk'), axis=0, tiled=True)]
    dot_general x44 -> x25, matrix products: 163 us -> 62.5 us  [the longest x7 18.9 us: dot_last(): lax.dot_general(a, b, (((1,), (1,)), ((), ())), preferred_element_type=F32)]
    unnamed x2 -> x0, blocking collectives: 81.7 us -> none
    unnamed x21 -> x0, waiting for transfers between devices: 78.1 us -> none
  transfers between devices with their start and end apart: 27 -> 16, of which waited for: 22 -> 3; matrix products, arithmetic and copies ran while one was open for 10% -> 25% of each run, Pallas kernels for 0% -> 66%
where the time goes in v1:
time: 579 us; the launch traced here: 571 us
  Pallas kernels  375 us (65%)
  matrix products  62.5 us (11%)
  local copies, waits for them, and re-layouts  56.7 us (10%)
  other arithmetic  46.1 us (8%)
  starting transfers between devices  18.2 us (3%)
  waiting for transfers between devices  10.6 us (2%)
    pallas_call x4, Pallas kernels, reduce_scatter_blk(): pl.pallas_call(functools.partial(rs_kernel, count, chips, plans), out_sha...  186 us
    pallas_call x4, Pallas kernels, all_gather_blk(): pl.pallas_call(functools.partial(ag_kernel, count, chips, plans), out_sha...  165 us
    unnamed x167, local copies, waits for them, and re-layouts  21.1 us
    dot_general x7, matrix products, dot_last(): lax.dot_general(a, b, (((1,), (1,)), ((), ())), preferred_element_type=F32)  18.9 us
    ppermute x16, starting transfers between devices, swap(): return lax.ppermute(array, 'head', [(0, 1), (1, 0)])  18.2 us
    dot_general x7, matrix products, dot_first(): lax.dot_general(a, b, (((0,), (0,)), ((), ())), preferred_element_type=F32)  16 us
    pallas_call x1, Pallas kernels, attention_backward(): pl.pallas_call(functools.partial(backward_kernel, repeats), grid_spec=plt...  14.1 us
    dot_general x7, matrix products, dot(): return jnp.dot(a, b, preferred_element_type=F32)  11.9 us
  transfers between devices with their start and end apart: 16, of which 3 were waited for; matrix products, arithmetic and copies ran while one was open for 25% of the time, Pallas kernels for 66%

profile of v1, /device:TPU:0, one launch (start us, length us, event | category | flops | bytes accessed | tf_op | source)
XLA Modules:
  0.0 570.9 jit_solution(9079125851805457684)
XLA Ops:
  17.9 5.6 collective-permute-done.2
  26.2 70.6 %shard_map.258 = (bf16[2,16,48,1024]{3,2,1,0:T(8,128)(2,1)}, bf16[16,48,1536]{2,1,0:T(8,128)(2,1)}, bf16[16,32,1536]{2,1,0:T(8,128)(2,1)}, bf16[16,128,1536]{2,1,0:T(8,128)(2,1)}) custom-call(bf16[2,48,1024]{2,1,0:T(8,128)(2,1)} %maximum_select_fusion.10.refs_0_, bf16[48,1536]{1,0:T(8,128)(2,1)} %refs_1_.1, bf16[32,1536]{1,0:T(8,128)(2,1)} %refs_2_.1, ...), custom_call_target="tpu_custom_call" | custom-call | tf_op jit(solution)/shard_map/pallas_call | solution.py:128
  97.6 28.6 %shard_map.255 = bf16[2,16,48,1408]{3,2,1,0:T(8,128)(2,1)} custom-call(bf16[2,48,1408]{2,1,0:T(8,128)(2,1)} %maximum_select_fusion.7.refs_0_), custom_call_target="tpu_custom_call" | custom-call | tf_op jit(solution)/shard_map/pallas_call | solution.py:128
  132.7 26.8 %shard_map.256 = bf16[16,256,512]{2,1,0:T(8,128)(2,1)} custom-call(bf16[256,512]{1,0:T(8,128)(2,1)} %slice.129.refs_0_), custom_call_target="tpu_custom_call" | custom-call | tf_op jit(solution)/shard_map/pallas_call | solution.py:128
  161.8 9.3 %shard_map.257 = (bf16[256,768]{1,0:T(8,128)(2,1)S(1)}, f32[256,768]{1,0:T(8,128)S(1)}, f32[2,2,384]{2,1,0:T(2,128)S(1)}) custom-call(s32[32]{0:T(128)S(1)} %select_reduce_fusion.slots_ref, s32[2]{0:T(128)S(1)} %dynamic_slice.82.places_ref, s32[3]{0:T(128)S(1)} %bitcast.173, bf16[256,768]{1,0:T(8,128)(2,1)S(1)} %slice.128.q_ref, ...), custom_call_target="tpu_custom_call" | custom-call | tf_op jit(solution)/shard_map/pallas_call | solution.py:389
  191.2 39.2 %shard_map.259 = bf16[16,128,1664]{2,1,0:T(8,128)(2,1)} custom-call(bf16[128,1664]{1,0:T(8,128)(2,1)} %concatenate.92.refs_0_), custom_call_target="tpu_custom_call" | custom-call | tf_op jit(solution)/shard_map/pallas_call | solution.py:128
  233.7 5.5 fusion.2
  239.1 4.7 copy.91
  244.3 3.9 convolution_convert_fusion.3
  265.9 3.7 fusion.87
  269.6 4.0 multiply_convert_fusion.2
  279.5 4.0 convolution_convert_fusion.5
  285.4 3.4 convolution_convert_fusion.4
  288.9 4.5 multiply_reduce_fusion
  293.9 3.4 pad_maximum_fusion.refs_0_
  297.4 46.6 %shard_map.261 = f32[128,1664]{1,0:T(8,128)} custom-call(bf16[16,128,1664]{2,1,0:T(8,128)(2,1)} %pad_maximum_fusion.refs_0_), custom_call_target="tpu_custom_call" | custom-call | tf_op jit(solution)/shard_map/pallas_call | solution.py:263
  350.8 3.5 fusion.14
  364.1 41.1 %shard_map.260 = f32[128,1536]{1,0:T(8,128)} custom-call(bf16[16,128,1536]{2,1,0:T(8,128)(2,1)} %get-tuple-element.97.refs_0_), custom_call_target="tpu_custom_call" | custom-call | tf_op jit(solution)/shard_map/pallas_call | solution.py:263
  410.8 14.1 %shard_map.262 = (bf16[256,768]{1,0:T(8,128)(2,1)}, bf16[32,128,256]{2,1,0:T(8,128)(2,1)}, bf16[32,128,256]{2,1,0:T(8,128)(2,1)}) custom-call(s32[32]{0:T(128)} %copy-done.4, s32[2]{0:T(128)} %copy-done.5, s32[3]{0:T(128)} %bitcast.174, bf16[256,768]{1,0:T(8,128)(2,1)} %copy-done.1, bf16[32,128,512]{2,1,0:T(8,128)(2,1)} %bitcast.168, ...), custom_call_target="tpu_custom_call" | custom-call | tf_op jit(solution)/shard_map/pallas_call | solution.py:454
  426.6 30.2 %shard_map.263 = (bf16[256,256]{1,0:T(8,128)(2,1)}, bf16[256,256]{1,0:T(8,128)(2,1)}) custom-call(bf16[16,256,256]{2,1,0:T(8,128)(2,1)} %bitcast.211, bf16[16,256,256]{2,1,0:T(8,128)(2,1)} %bitcast.212), custom_call_target="tpu_custom_call" | custom-call | tf_op jit(solution)/shard_map/pallas_call | solution.py:263
  460.0 3.6 fusion.5
  469.4 3.6 collective-permute-done.11
  477.6 68.0 %shard_map.264 = (bf16[2,48,1280]{2,1,0:T(8,128)(2,1)}, bf16[2,48,1024]{2,1,0:T(8,128)(2,1)}, f32[48,1536]{1,0:T(8,128)}, f32[32,1536]{1,0:T(8,128)}, f32[2,48,128]{2,1,0:T(8,128)}) custom-call(bf16[2,16,48,1280]{3,2,1,0:T(8,128)(2,1)} %bitcast.175, bf16[2,16,48,1024]{3,2,1,0:T(8,128)(2,1)} %bitcast.178, bf16[16,48,1536]{2,1,0:T(8,128)(2,1)} %bitcast.183, ...), custom_call_target="tpu_custom_call" | custom-call | tf_op jit(solution)/shard_map/pallas_call | solution.py:263
  564.2 4.9 fusion.9
  (308 shorter events, 136.0 us)
Async XLA Ops:
  5.5 91.3 %collective-permute-start.1 = (bf16[48,1408]{1,0:T(8,128)(2,1)S(1)}, bf16[48,1408]{1,0:T(8,128)(2,1)S(1)}, u32[]{:S(2)}, u32[]{:S(2)}) collective-permute-start(bf16[48,1408]{1,0:T(8,128)(2,1)S(1)} %concatenate.91), channel_id=1, source_target_pairs={{0,16},{16,0},{1,17},{17,1},{2,18},{18,2},{3,19},{19,3},{4,20},{20... | collective-permute-start | bytes 405512 | tf_op jit(solution)/shard_map/ppermute | solution.py:320
  8.5 120.0 %collective-permute-start = (bf16[128,1536]{1,0:T(8,128)(2,1)}, bf16[128,1536]{1,0:T(8,128)(2,1)S(1)}, u32[]{:S(2)}, u32[]{:S(2)}) collective-permute-start(bf16[128,1536]{1,0:T(8,128)(2,1)} %param.16), channel_id=1, source_target_pairs={{0,16},{16,0},{1,17},{17,1},{2,18},{18,2},{3,19},{19,3},{4,20},{20... | collective-permute-start | bytes 1179656 | tf_op jit(solution)/shard_map/ppermute | solution.py:320
  9.9 13.6 %collective-permute-start.2 = (bf16[48,1024]{1,0:T(8,128)(2,1)S(1)}, bf16[48,1024]{1,0:T(8,128)(2,1)S(1)}, u32[]{:S(2)}, u32[]{:S(2)}) collective-permute-start(bf16[48,1024]{1,0:T(8,128)(2,1)S(1)} %bitcast.227), channel_id=1, source_target_pairs={{0,16},{16,0},{1,17},{17,1},{2,18},{18,2},{3,19},{19,3},{4,20},{20... | collective-permute-start | bytes 294920 | tf_op jit(solution)/shard_map/ppermute | solution.py:320
  11.9 251.2 %collective-permute-start.4 = (bf16[768,1024]{1,0:T(8,128)(2,1)}, bf16[768,1024]{1,0:T(8,128)(2,1)}, u32[]{:S(2)}, u32[]{:S(2)}) collective-permute-start(bf16[768,1024]{1,0:T(8,128)(2,1)} %bitcast.216), channel_id=1, source_target_pairs={{0,16},{16,0},{1,17},{17,1},{2,18},{18,2},{3,19},{19,3},{4,20},{20... | collective-permute-start | bytes 4718600 | tf_op jit(solution)/shard_map/ppermute | solution.py:320
  12.0 257.7 %collective-permute-start.5 = (bf16[512,768]{1,0:T(8,128)(2,1)}, bf16[512,768]{1,0:T(8,128)(2,1)}, u32[]{:S(2)}, u32[]{:S(2)}) collective-permute-start(bf16[512,768]{1,0:T(8,128)(2,1)} %bitcast.232), channel_id=1, source_target_pairs={{0,16},{16,0},{1,17},{17,1},{2,18},{18,2},{3,19},{19,3},{4,20},{20... | collective-permute-start | bytes 2359304 | tf_op jit(solution)/shard_map/ppermute | solution.py:320
  14.9 144.6 %copy-start.4 = (s32[32]{0:T(128)}, s32[32]{0:T(128)S(1)}, u32[]{:S(2)}) copy-start(s32[32]{0:T(128)S(1)} %select_reduce_fusion.slots_ref) | copy-start | bytes 388
  16.9 142.7 %copy-start.5 = (s32[2]{0:T(128)}, s32[2]{0:T(128)S(1)}, u32[]{:S(2)}) copy-start(s32[2]{0:T(128)S(1)} %dynamic_slice.82.places_ref) | copy-start | bytes 28
  17.7 141.9 %copy-start.6 = (s32[3,1]{0,1:T(1,128)}, s32[3,1]{0,1:T(1,128)S(1)}, u32[]{:S(2)}) copy-start(s32[3,1]{0,1:T(1,128)S(1)} %reduce-window.9) | copy-start | bytes 40
  23.5 156.7 %collective-permute-start.8 = (bf16[128,1536]{1,0:T(8,128)(2,1)}, bf16[128,1536]{1,0:T(8,128)(2,1)}, u32[]{:S(2)}, u32[]{:S(2)}) collective-permute-start(bf16[128,1536]{1,0:T(8,128)(2,1)} %refs_3_.1), channel_id=1, source_target_pairs={{0,16},{16,0},{1,17},{17,1},{2,18},{18,2},{3,19},{19,3},{4,20},{20... | collective-permute-start | bytes 1179656 | tf_op jit(solution)/shard_map/ppermute | solution.py:320
  173.4 10.3 %collective-permute-start.3 = (bf16[128,1536]{1,0:T(8,128)(2,1)S(1)}, bf16[128,1536]{1,0:T(8,128)(2,1)}, u32[]{:S(2)}, u32[]{:S(2)}) collective-permute-start(bf16[128,1536]{1,0:T(8,128)(2,1)S(1)} %fusion.51), channel_id=1, source_target_pairs={{0,16},{16,0},{1,17},{17,1},{2,18},{18,2},{3,19},{19,3},{4,20},{20... | collective-permute-start | bytes 1179656 | tf_op jit(solution)/shard_map/ppermute | solution.py:320
  186.6 61.7 %collective-permute-start.6 = (bf16[128,1536]{1,0:T(8,128)(2,1)S(1)}, bf16[128,1536]{1,0:T(8,128)(2,1)S(1)}, u32[]{:S(2)}, u32[]{:S(2)}) collective-permute-start(bf16[128,1536]{1,0:T(8,128)(2,1)S(1)} %multiply_convert_fusion.4), channel_id=1, source_target_pairs={{0,16},{16,0},{1,17},{17,1},{2,18},{18,2},{3,19},{19,3},{4,20},{20... | collective-permute-start | bytes 1179656 | tf_op jit(solution)/shard_map/ppermute | solution.py:320
  254.1 92.1 %collective-permute-start.9 = (bf16[128,1536]{1,0:T(8,128)(2,1)}, bf16[128,1536]{1,0:T(8,128)(2,1)}, u32[]{:S(2)}, u32[]{:S(2)}) collective-permute-start(bf16[128,1536]{1,0:T(8,128)(2,1)} %fusion.53), channel_id=1, source_target_pairs={{0,16},{16,0},{1,17},{17,1},{2,18},{18,2},{3,19},{19,3},{4,20},{20... | collective-permute-start | bytes 1179656 | tf_op jit(solution)/shard_map/ppermute | solution.py:320
  258.2 297.1 %collective-permute-start.7 = (bf16[128,1536]{1,0:T(8,128)(2,1)}, bf16[128,1536]{1,0:T(8,128)(2,1)}, u32[]{:S(2)}, u32[]{:S(2)}) collective-permute-start(bf16[128,1536]{1,0:T(8,128)(2,1)} %fusion.52), channel_id=1, source_target_pairs={{0,16},{16,0},{1,17},{17,1},{2,18},{18,2},{3,19},{19,3},{4,20},{20... | collective-permute-start | bytes 1179656 | tf_op jit(solution)/shard_map/ppermute | solution.py:320
  278.0 274.7 %collective-permute-start.15 = (bf16[512,768]{1,0:T(8,128)(2,1)}, bf16[512,768]{1,0:T(8,128)(2,1)}, u32[]{:S(2)}, u32[]{:S(2)}) collective-permute-start(bf16[512,768]{1,0:T(8,128)(2,1)} %fusion.34), channel_id=1, source_target_pairs={{0,16},{16,0},{1,17},{17,1},{2,18},{18,2},{3,19},{19,3},{4,20},{20... | collective-permute-start | bytes 2359304 | tf_op jit(solution)/shard_map/ppermute | solution.py:320
  297.3 46.6 %copy-start.62 = (f32[128]{0:T(128)S(1)}, f32[128]{0:T(128)}, u32[]{:S(2)}) copy-start(f32[128]{0:T(128)} %copy-done.61) | copy-start | bytes 1540
  297.4 46.6 %copy-start.64 = (f32[128]{0:T(128)S(1)}, f32[128]{0:T(128)}, u32[]{:S(2)}) copy-start(f32[128]{0:T(128)} %copy-done.63) | copy-start | bytes 1540
  297.4 48.9 %copy-start.45 = (f32[1536]{0:T(1024)S(1)}, f32[1536]{0:T(1024)}, u32[]{:S(2)}) copy-start(f32[1536]{0:T(1024)} %copy-done.44) | copy-start | bytes 18436
  297.4 48.9 %copy-start.59 = (f32[128]{0:T(128)S(1)}, f32[128]{0:T(128)}, u32[]{:S(2)}) copy-start(f32[128]{0:T(128)} %copy-done.58) | copy-start | bytes 1540
  350.5 54.7 %collective-permute-start.10 = (bf16[128,1536]{1,0:T(8,128)(2,1)}, bf16[128,1536]{1,0:T(8,128)(2,1)}, u32[]{:S(2)}, u32[]{:S(2)}) collective-permute-start(bf16[128,1536]{1,0:T(8,128)(2,1)} %fusion.81), channel_id=1, source_target_pairs={{0,16},{16,0},{1,17},{17,1},{2,18},{18,2},{3,19},{19,3},{4,20},{20... | collective-permute-start | bytes 1179656 | tf_op jit(solution)/shard_map/ppermute | solution.py:320
  358.3 205.9 %collective-permute-start.14 = (bf16[768,1024]{1,0:T(8,128)(2,1)}, bf16[768,1024]{1,0:T(8,128)(2,1)}, u32[]{:S(2)}, u32[]{:S(2)}) collective-permute-start(bf16[768,1024]{1,0:T(8,128)(2,1)} %fusion.16), channel_id=1, source_target_pairs={{0,16},{16,0},{1,17},{17,1},{2,18},{18,2},{3,19},{19,3},{4,20},{20... | collective-permute-start | bytes 4718600 | tf_op jit(solution)/shard_map/ppermute | solution.py:320
  463.7 9.3 %collective-permute-start.11 = (bf16[128,1536]{1,0:T(8,128)(2,1)S(1)}, bf16[128,1536]{1,0:T(8,128)(2,1)S(1)}, u32[]{:S(2)}, u32[]{:S(2)}) collective-permute-start(bf16[128,1536]{1,0:T(8,128)(2,1)S(1)} %fusion.54), channel_id=1, source_target_pairs={{0,16},{16,0},{1,17},{17,1},{2,18},{18,2},{3,19},{19,3},{4,20},{20... | collective-permute-start | bytes 1179656 | tf_op jit(solution)/shard_map/ppermute | solution.py:320
  477.6 74.5 %copy-start.68 = (f32[128]{0:T(128)S(1)}, f32[128]{0:T(128)}, u32[]{:S(2)}) copy-start(f32[128]{0:T(128)} %get-tuple-element.87) | copy-start | bytes 1540
  548.4 11.0 %collective-permute-start.13 = (bf16[48,2304]{1,0:T(8,128)(2,1)}, bf16[48,2304]{1,0:T(8,128)(2,1)}, u32[]{:S(2)}, u32[]{:S(2)}) collective-permute-start(bf16[48,2304]{1,0:T(8,128)(2,1)} %pad_maximum_fusion.5), channel_id=1, source_target_pairs={{0,16},{16,0},{1,17},{17,1},{2,18},{18,2},{3,19},{19,3},{4,20},{20... | collective-permute-start | bytes 663560 | tf_op jit(solution)/shard_map/ppermute | solution.py:320
  551.0 7.0 %collective-permute-start.12 = (f32[48,128]{1,0:T(8,128)S(1)}, f32[48,128]{1,0:T(8,128)S(1)}, u32[]{:S(2)}, u32[]{:S(2)}) collective-permute-start(f32[48,128]{1,0:T(8,128)S(1)} %dynamic-slice_bitcast_fusion.4), channel_id=1, source_target_pairs={{0,16},{16,0},{1,17},{17,1},{2,18},{18,2},{3,19},{19,3},{4,20},{20... | collective-permute-start | bytes 73736 | tf_op jit(solution)/shard_map/ppermute | solution.py:320
  (71 other events, 495.5 us)

commit v2 on v1

--- a/solution.py
+++ b/solution.py
@@ -468,6 +468,403 @@
     )(*where, query, kv, kv, full, grad, lse)
 
 
+def tiles(total, size, body):
+    if total == size:
+        body(pl.ds(0, size))
+    else:
+
+        @pl.loop(0, total // size)
+        def _(i):
+            body(pl.ds(pl.multiple_of(i * size, size), size))
+
+
+def shifted(c, by):
+    if isinstance(c.start, int):
+        return pl.ds(c.start + by, c.size)
+    return pl.ds(pl.multiple_of(c.start + by, c.size), c.size)
+
+
+def expert_kernel(
+    chips, experts, ext_ref, in_ref, out_ref, cot_ref,
+    home_ref, routed_ref, din_ref, dout_ref,
+    ext, cot, rows_x, rows_dy, rows_act, rows_dab, both, result, back, deal, gate,
+    own_d, own_o, stage_d, stage_o, sib_d, sib_o, right_d, right_o, left_d, left_o,
+    copy_sem, cot_sem, ag_r, ag_l, ag_sr, ag_sl, ss_r, ss_l, ss_sr, ss_sl,
+    ex_sem, ss_ex, rs_r, rs_l, ss_rr, ss_rl,
+):
+    blk, core, at, sib = ring_info(chips)
+    right, left = at(1), at(-1)
+    half = chips // 2
+    rows, wide = ext_ref.shape
+    width = in_ref.shape[0]
+    hidden = out_ref.shape[0]
+    slots = rows_x.shape[0] // chips
+    cut = rows // 2
+    upper, lower = pl.ds(0, cut), pl.ds(cut, cut)
+
+    barrier = pltpu.get_barrier_semaphore()
+    for other in (right, left, sib):
+        pl.semaphore_signal(barrier, inc=1, device_id={"blk": other}, device_id_type=MESH)
+    pl.semaphore_wait(barrier, 3)
+
+    def remote(src, dst, ssem, rsem, dev):
+        return pltpu.make_async_remote_copy(
+            src_ref=src, dst_ref=dst, send_sem=ssem, recv_sem=rsem,
+            device_id={"blk": dev}, device_id_type=MESH)
+
+    def hop_right(part, k, s):
+        ref = ext.at[at(1 - s), part]
+        return remote(ref, ref, ss_r.at[k, s], ag_r.at[k, s], right)
+
+    def hop_left(part, k, s):
+        ref = ext.at[at(s - 1), part]
+        return remote(ref, ref, ss_l.at[k, s], ag_l.at[k, s], left)
+
+    def over_right(part, k, s):
+        ref = ext.at[at(-s), part]
+        return remote(ref, ref, ss_sr.at[k, s], ag_sr.at[k, s], sib)
+
+    def over_left(part, k, s):
+        ref = ext.at[at(s), part]
+        return remote(ref, ref, ss_sl.at[k, s], ag_sl.at[k, s], sib)
+
+    def cot_copy(g, j):
+        there = at(-g) if j == 0 else at(g + 1)
+        slot = lax.rem(g, 2)
+        return pltpu.make_async_copy(
+            cot_ref.at[pl.ds(there - core, 2)], cot.at[slot, j], cot_sem.at[slot, j])
+
+    def place_of(g, j):
+        return at(-g) if j == 0 else at(g + 1)
+
+    def exchange_d(g, j):
+        return remote(stage_d.at[j], sib_d.at[lax.div(place_of(g, j), 2)], ss_ex.at[0, j, g], ex_sem.at[0, j, g], sib)
+
+    def exchange_o(g, j):
+        return remote(stage_o.at[j], sib_o.at[lax.div(place_of(g, j), 2)], ss_ex.at[1, j, g], ex_sem.at[1, j, g], sib)
+
+    mine = pltpu.make_async_copy(ext_ref, ext.at[blk], copy_sem)
+    mine.start()
+    cot_copy(0, 0).start()
+    cot_copy(0, 1).start()
+    mine.wait()
+    for k, part in ((0, upper), (1, lower)):
+        hop_right(part, k, 1).start()
+        hop_left(part, k, 1).start()
+        over_right(part, k, 0).start()
+
+    triangle = lax.broadcasted_iota(jnp.int32, (rows, rows), 0) > lax.broadcasted_iota(jnp.int32, (rows, rows), 1)
+    triangle = triangle.astype(BF16)
+    lane = lax.broadcasted_iota(jnp.int32, (rows, 128), 1)
+
+    @pl.loop(0, half)
+    def _(g):
+        s = g + 1
+        hop_right(upper, 0, s).wait_recv()
+
+        @pl.when(s < half)
+        def _():
+            hop_right(upper, 0, s + 1).start()
+
+        over_right(upper, 0, s).start()
+        hop_left(lower, 1, s).wait_recv()
+
+        @pl.when(s < half)
+        def _():
+            hop_left(lower, 1, s + 1).start()
+
+        over_left(lower, 1, s).start()
+
+        @pl.when(s < half)
+        def _():
+            hop_right(lower, 1, s).wait_recv()
+
+            @pl.when(s < half - 1)
+            def _():
+                hop_right(lower, 1, s + 1).start()
+
+            over_right(lower, 1, s).start()
+            hop_left(upper, 0, s).wait_recv()
+
+            @pl.when(s < half - 1)
+            def _():
+                hop_left(upper, 0, s + 1).start()
+
+            over_left(upper, 0, s).start()
+
+        over_right(upper, 0, g).wait_recv()
+        over_right(lower, 1, g).wait_recv()
+        over_left(lower, 1, s).wait_recv()
+
+        @pl.when(s < half)
+        def _():
+            over_left(upper, 0, s).wait_recv()
+
+        @pl.when(s == half)
+        def _():
+            over_right(upper, 0, s).wait_recv()
+
+        cot_copy(g, 0).wait()
+        cot_copy(g, 1).wait()
+
+        @pl.when(s < half)
+        def _():
+            cot_copy(g + 1, 0).start()
+            cot_copy(g + 1, 1).start()
+
+        turn = lax.rem(g, 2)
+        group = pl.ds(pl.multiple_of(g * 2 * slots, 2 * slots), 2 * slots)
+        firsts = (at(-g) - core, at(g + 1) - core)
+        for j in range(2):
+            for i in range(2):
+                lanes = ext[firsts[j] + i, :, pl.ds(width, 128)].astype(F32)
+                chosen = jnp.sum(jnp.where(lane == experts + blk, lanes, 0.0), axis=1, keepdims=True)
+                weight = jnp.sum(jnp.where(lane == blk, lanes, 0.0), axis=1, keepdims=True)
+                chosen = jnp.broadcast_to(chosen, (rows, 128))
+                rank = dot(triangle, chosen.astype(BF16)) + i * (slots // 2)
+                spread = jnp.where((rank == lane.astype(F32)) & (chosen > 0.5), 1.0, 0.0)
+                deal[j, i] = spread.astype(BF16)
+                gate[j, i] = jnp.broadcast_to(weight, (rows, 128))
+            where = pl.ds(pl.multiple_of(g * 2 * slots + j * slots, slots), slots)
+
+            def pick_rows(c, j=j, where=where):
+                taken = dot_first(deal[j, 0], ext[firsts[j], :, c]) + dot_first(deal[j, 1], ext[firsts[j] + 1, :, c])
+                rows_x[where, c] = taken.astype(BF16)
+                scaled = [(deal[j, i] * gate[j, i].astype(BF16)) for i in range(2)]
+                taken = dot_first(scaled[0], cot[turn, j, 0, :, c]) + dot_first(scaled[1], cot[turn, j, 1, :, c])
+                rows_dy[where, c] = taken.astype(BF16)
+
+            tiles(width, 512, pick_rows)
+
+        def hidden_tile(c):
+            high = shifted(c, hidden)
+            x = rows_x[group]
+            gate_part = dot(x, in_ref[:, c])
+            lift = dot(x, in_ref[:, high])
+            both[:, c] = gate_part
+            both[:, high] = lift
+            rows_act[group, c] = (jax.nn.silu(gate_part) * lift).astype(BF16)
+
+        tiles(hidden, 256, hidden_tile)
+
+        def result_tile(c):
+            result[:, c] = dot(rows_act[group], out_ref[:, c]).astype(BF16)
+
+        tiles(width, 512, result_tile)
+
+        def grad_tile(c):
+            high = shifted(c, hidden)
+            da = dot_last(rows_dy[group], out_ref[c, :])
+            gate_part, lift = both[:, c], both[:, high]
+            sig = jax.nn.sigmoid(gate_part)
+            rows_dab[group, c] = (da * lift * sig * (1.0 + gate_part * (1.0 - sig))).astype(BF16)
+            rows_dab[group, high] = (da * gate_part * sig).astype(BF16)
+
+        tiles(hidden, 256, grad_tile)
+
+        def back_tile(c):
+            back[:, c] = dot_last(rows_dab[group], in_ref[c, :]).astype(BF16)
+
+        tiles(width, 512, back_tile)
+
+        @pl.when(g > 0)
+        def _():
+            for j in range(2):
+                exchange_d(g - 1, j).wait_send()
+                exchange_o(g - 1, j).wait_send()
+
+        for j in range(2):
+            chip = lax.div(firsts[j], 2)
+            for which, to_d, to_o in (
+                (core, own_d.at[chip], own_o.at[chip]),
+                (1 - core, stage_d.at[j], stage_o.at[j]),
+            ):
+                part = pl.ds(j * slots, slots)
+                dealer = deal[j, which]
+                share = gate[j, which]
+                total = jnp.zeros((rows, 1), F32)
+                for t in range(width // 512):
+                    c = pl.ds(t * 512, 512)
+                    home_rows = dot(dealer, result[part, c])
+                    to_o[:, c] = (home_rows * share[:, :1]).astype(BF16)
+                    total = total + jnp.sum(
+                        home_rows * cot[turn, j, which, :, c].astype(F32), axis=1, keepdims=True)
+                    to_d[:, c] = dot(dealer, back[part, c]).astype(BF16)
+                high = total.astype(BF16).astype(F32)
+                lanes = jnp.where(lane == blk, high, jnp.where(lane == experts + blk, total - high, 0.0))
+                to_d[:, pl.ds(width, 128)] = lanes.astype(BF16)
+            exchange_d(g, j).start()
+            exchange_o(g, j).start()
+
+    arrays = ((0, own_d, sib_d, right_d, left_d, home_ref), (1, own_o, sib_o, right_o, left_o, routed_ref))
+    arrived = set()
+
+    def join(a, own, other, d, part, into, received):
+        g, j = (d - 1, 1) if d > 0 else (-d, 0)
+        if (a, g, j) not in arrived:
+            arrived.add((a, g, j))
+            (exchange_d, exchange_o)[a](g, j).wait_recv()
+        chip = lax.div(at(d), 2)
+
+        def add(c):
+            total = own[chip, c].astype(F32) + other[chip, c].astype(F32)
+            for ref in received:
+                total = total + ref[c].astype(F32)
+            into[c] = total.astype(into.dtype)
+
+        @pl.loop(0, cut // 16)
+        def _(i):
+            add(pl.ds(pl.multiple_of(part.start + i * 16, 16), 16))
+
+    def pass_right(a, src, buf, k, part, s):
+        return remote(src.at[part], buf.at[s - 1, part], ss_rr.at[a, k, s], rs_r.at[a, k, s], right)
+
+    def pass_left(a, src, buf, k, part, s):
+        return remote(src.at[part], buf.at[s - 1, part], ss_rl.at[a, k, s], rs_l.at[a, k, s], left)
+
+    ways = (
+        (0, upper, 1, half), (1, lower, -1, half), (1, lower, 1, half - 1), (0, upper, -1, half - 1),
+    )
+    sent = []
+    for s in range(1, half + 1):
+        for a, own, other, to_right, to_left, _ in arrays:
+            for k, part, way, hops in ways:
+                if s > hops:
+                    continue
+                make, buf = (pass_right, to_right) if way > 0 else (pass_left, to_left)
+                d = way * (hops - s + 1)
+                if d == -half:
+                    d = half
+                if s == 1:
+                    src = own.at[lax.div(at(d), 2)]
+                    join(a, own, other, d, part, src, ())
+                else:
+                    src = buf.at[s - 2]
+                    make(a, src, buf, k, part, s - 1).wait_recv()
+                    join(a, own, other, d, part, src, (src,))
+                copy = make(a, src, buf, k, part, s)
+                copy.start()
+                sent.append(copy)
+        if s < half:
+            each = width // 256 // (half - 1)
+
+            @pl.loop((s - 1) * each, s * each)
+            def _(i):
+                c = pl.ds(pl.multiple_of(i * 256, 256), 256)
+                din_ref[c, :] = dot_first(rows_x[:, c], rows_dab[...]).astype(BF16)
+        else:
+
+            def weight_tile(c):
+                dout_ref[c, :] = dot_first(rows_act[:, c], rows_dy[...]).astype(BF16)
+
+            tiles(hidden, 256, weight_tile)
+    for a, own, other, to_right, to_left, into in arrays:
+        for k, part in ((0, upper), (1, lower)):
+            last_right, last_left = half - k, half - 1 + k
+            pass_right(a, own.at[0], to_right, k, part, last_right).wait_recv()
+            pass_left(a, own.at[0], to_left, k, part, last_left).wait_recv()
+            join(a, own, other, 0, part, into, (to_right.at[last_right - 1], to_left.at[last_left - 1]))
+    for copy in sent:
+        copy.wait_send()
+    for j in range(2):
+        exchange_d(half - 1, j).wait_send()
+        exchange_o(half - 1, j).wait_send()
+    for k, part in ((0, upper), (1, lower)):
+        over_right(part, k, 0).wait_send()
+        for s in range(1, half + 1):
+            if s <= half - k:
+                hop_right(part, k, s).wait_send()
+                over_right(part, k, s).wait_send()
+            if s <= half - 1 + k:
+                hop_left(part, k, s).wait_send()
+                over_left(part, k, s).wait_send()
+
+
+def experts_fused(ext, expert_in, expert_out, cot_all, blks, capacity, collective_id):
+    chips, half = blks // 2, blks // 4
+    rows, wide = ext.shape
+    width, hidden = expert_in.shape[0], expert_out.shape[0]
+    count = blks * capacity
+    group = 4 * capacity
+    dma = pltpu.SemaphoreType.DMA
+    vmem = pl.BlockSpec(memory_space=pltpu.VMEM)
+    anywhere = pl.BlockSpec(memory_space=pl.ANY)
+
+    def low(*shape):
+        return pltpu.VMEM(shape, BF16)
+
+    return pl.pallas_call(
+        functools.partial(expert_kernel, chips, blks),
+        out_shape=[
+            jax.ShapeDtypeStruct((rows, wide), F32), jax.ShapeDtypeStruct((rows, width), F32),
+            jax.ShapeDtypeStruct(expert_in.shape, BF16), jax.ShapeDtypeStruct(expert_out.shape, BF16),
+        ],
+        in_specs=[anywhere, vmem, vmem, anywhere],
+        out_specs=[vmem] * 4,
+        scratch_shapes=[
+            low(blks, rows, wide), low(2, 2, 2, rows, width),
+            low(count, width), low(count, width), low(count, hidden), low(count, 2 * hidden),
+            pltpu.VMEM((group, 2 * hidden), F32), low(group, width), low(group, width),
+            low(2, 2, rows, 128), pltpu.VMEM((2, 2, rows, 128), F32),
+            low(chips, rows, wide), low(chips, rows, width), low(2, rows, wide), low(2, rows, width),
+            low(chips, rows, wide), low(chips, rows, width),
+            low(half, rows, wide), low(half, rows, width), low(half, rows, wide), low(half, rows, width),
+            dma(()), dma((2, 2)),
+            dma((2, half + 1)), dma((2, half + 1)), dma((2, half + 1)), dma((2, half + 1)),
+            dma((2, half + 1)), dma((2, half + 1)), dma((2, half + 1)), dma((2, half + 1)),
+            dma((2, 2, half)), dma((2, 2, half)),
+            dma((2, 2, half + 1)), dma((2, 2, half + 1)), dma((2, 2, half + 1)), dma((2, 2, half + 1)),
+        ],
+        compiler_params=pltpu.CompilerParams(
+            collective_id=collective_id, has_side_effects=True, vmem_limit_bytes=62 << 20),
+    )(ext, expert_in, expert_out, cot_all)
+
+
+def experts_plain(own_ext, expert_in, expert_out, cot_all, blks, capacity, collective_id):
+    b = lax.axis_index("blk")
+    experts, width = blks, expert_in.shape[0]
+    rows = own_ext.shape[0]
+    ext = all_gather_blk([own_ext], blks, collective_id)[0]
+    norm_all = ext[:, :, :width]
+    gate_here = lax.dynamic_index_in_dim(ext, width + b, 2, keepdims=False).astype(F32)
+    mask_here = lax.dynamic_index_in_dim(ext, width + experts + b, 2, keepdims=False).astype(F32)
+    rank = jnp.cumsum(mask_here, axis=1) - mask_here
+    slots = jnp.arange(capacity, dtype=F32)
+    deal = ((rank[:, None, :] == slots[None, :, None]) & (mask_here[:, None, :] > 0)).astype(BF16)
+    deal_gate = deal * gate_here[:, None, :].astype(BF16)
+
+    def to_slots(dealer, array):
+        moved = jnp.einsum("bst,btd->bsd", dealer, array, preferred_element_type=F32)
+        return moved.astype(BF16).reshape(blks * capacity, width)
+
+    def to_rows(dealer, array):
+        return jnp.einsum(
+            "bst,bsd->btd", dealer, array.reshape(blks, capacity, width), preferred_element_type=F32)
+
+    expert_rows = to_slots(deal, norm_all)
+    both = dot(expert_rows, expert_in)
+    ew = expert_out.shape[0]
+    gate_part, up_part = both[:, :ew], both[:, ew:]
+    activated = (jax.nn.silu(gate_part) * up_part).astype(BF16)
+    result = dot(activated, expert_out).astype(BF16)
+    result_rows = to_rows(deal, result)
+    gate_grad = jnp.sum(result_rows * cot_all.astype(F32), axis=2, keepdims=True)
+    routed = (result_rows * gate_here[:, :, None]).astype(BF16)
+    slot_grad = to_slots(deal_gate, cot_all)
+    act_grad = dot_last(slot_grad, expert_out)
+    both_grad = gated_grad(act_grad, gate_part, up_part)
+    rows_back = to_rows(deal, dot_last(both_grad, expert_in).astype(BF16)).astype(BF16)
+    lane = jnp.arange(128 * (-(-2 * experts // 128)), dtype=jnp.int32)
+    grad_high = gate_grad.astype(BF16)
+    grad_low = (gate_grad - grad_high.astype(F32)).astype(BF16)
+    grad_lanes = jnp.where(lane == b, grad_high, jnp.where(lane == b + experts, grad_low, jnp.zeros((), BF16)))
+    dwn = dot_first(activated, slot_grad).astype(BF16)
+    dup = dot_first(expert_rows, both_grad).astype(BF16)
+    home = reduce_scatter_blk([jnp.concatenate([rows_back, grad_lanes], axis=2)], blks, collective_id + 1, [F32])[0]
+    routed_sum = reduce_scatter_blk([routed], blks, collective_id + 2, [F32])[0]
+    return home, routed_sum, dup, dwn
+
+
 def shards(
     tokens, cotangent, seq_lengths, piece_order, routes, norm1_gain, w_query, w_key, w_value, w_out,
     norm2_gain, w_router, shared_up, shared_down, expert_up, expert_down,
@@ -553,47 +950,14 @@
     extra = jnp.concatenate(
         [gates.astype(BF16), mask.astype(BF16), jnp.zeros((rows, -2 * experts % 128), BF16)], axis=1)
 
-    ext = all_gather_blk([jnp.concatenate([normed_two, extra], axis=1)], blks, 3)[0]
-    norm_all = ext[:, :, :width]
-    gate_here = lax.dynamic_index_in_dim(ext, width + b, 2, keepdims=False).astype(F32)
-    mask_here = lax.dynamic_index_in_dim(ext, width + experts + b, 2, keepdims=False).astype(F32)
-    rank = jnp.cumsum(mask_here, axis=1) - mask_here
-    slots = jnp.arange(capacity, dtype=F32)
-    deal = ((rank[:, None, :] == slots[None, :, None]) & (mask_here[:, None, :] > 0)).astype(BF16)
-    deal_gate = deal * gate_here[:, None, :].astype(BF16)
-
-    def to_slots(dealer, array):
-        moved = jnp.einsum("bst,btd->bsd", dealer, array, preferred_element_type=F32)
-        return moved.astype(BF16).reshape(blks * capacity, width)
-
-    def to_rows(dealer, array):
-        return jnp.einsum(
-            "bst,bsd->btd", dealer, array.reshape(blks, capacity, width), preferred_element_type=F32)
-
-    expert_rows = to_slots(deal, norm_all)
-    both = dot(expert_rows, expert_in)
-    ew = expert_out.shape[0]
-    gate_part, up_part = both[:, :ew], both[:, ew:]
-    activated = (jax.nn.silu(gate_part) * up_part).astype(BF16)
-    result = dot(activated, expert_out).astype(BF16)
-    result_rows = to_rows(deal, result)
-    gate_grad = jnp.sum(result_rows * cot_all.astype(F32), axis=2, keepdims=True)
-    routed = (result_rows * gate_here[:, :, None]).astype(BF16)
-    slot_grad = to_slots(deal_gate, cot_all)
-    act_grad = dot_last(slot_grad, expert_out)
-    both_grad = gated_grad(act_grad, gate_part, up_part)
-    rows_back = to_rows(deal, dot_last(both_grad, expert_in).astype(BF16)).astype(BF16)
-    lane = jnp.arange(128 * (-(-2 * experts // 128)), dtype=jnp.int32)
-    grad_high = gate_grad.astype(BF16)
-    grad_low = (gate_grad - grad_high.astype(F32)).astype(BF16)
-    grad_lanes = jnp.where(lane == b, grad_high, jnp.where(lane == b + experts, grad_low, jnp.zeros((), BF16)))
-    home = reduce_scatter_blk([jnp.concatenate([rows_back, grad_lanes], axis=2)], blks, 4, [F32])[0]
-    routed_sum = reduce_scatter_blk([routed], blks, 5, [F32])[0]
-    dwn = dot_first(activated, slot_grad)
-    dup = dot_first(expert_rows, both_grad).reshape(2, width // 2, -1)
+    ext = jnp.concatenate([normed_two, extra], axis=1)
+    fits = blks == 16 and rows == 128 and 2 * capacity == 128 and width % 768 == 0
+    experts_run = experts_fused if fits else experts_plain
+    home, routed_sum, dup, dwn = experts_run(ext, expert_in, expert_out, cot_all, blks, capacity, 3)
+    dup = dup.reshape(2, width // 2, -1)
     dwn = jnp.stack([dwn[:, : width // 2], dwn[:, width // 2 :]])
-    expert_up_grad = pick(dup, h) + swap(pick(dup, 1 - h).astype(BF16)).astype(F32)
-    expert_down_grad = pick(dwn, h) + swap(pick(dwn, 1 - h).astype(BF16)).astype(F32)
+    expert_up_grad = pick(dup, h).astype(F32) + swap(pick(dup, 1 - h)).astype(F32)
+    expert_down_grad = pick(dwn, h).astype(F32) + swap(pick(dwn, 1 - h)).astype(F32)
 
     shared_both = dot(normed_pair, full_up)
     shared_gate, shared_lift = shared_both[:, :shared_width], shared_both[:, shared_width:]

time: 579 us -> 535 us (0.924)
  matrix products: 62.5 us -> 25.4 us
  local copies, waits for them, and re-layouts: 56.7 us -> 39.3 us
  waiting for transfers between devices: 10.6 us -> 26.4 us
  Pallas kernels: 375 us -> 383 us
  other arithmetic: 46.1 us -> 38.4 us
    pallas_call x0 -> x1, Pallas kernels: none -> 133 us  [experts_fused(): pl.pallas_call(functools.partial(expert_kernel, chips, blks), out_shape=[...]
    pallas_call x4 -> x2, Pallas kernels: 186 us -> 95.4 us  [reduce_scatter_blk(): pl.pallas_call(functools.partial(rs_kernel, count, chips, plans), out_sha...]
    pallas_call x4 -> x3, Pallas kernels: 165 us -> 126 us  [all_gather_blk(): pl.pallas_call(functools.partial(ag_kernel, count, chips, plans), out_sha...]
    ppermute x16, waiting for transfers between devices: 10.6 us -> 26.4 us  [swap(): return lax.ppermute(array, 'head', [(0, 1), (1, 0)])]
    dot_general x4 -> x0, matrix products: 15.7 us -> none  [the longest x2 9.38 us: to_slots(): jnp.einsum('bst,btd->bsd', dealer, array, preferred_element_type=F32)]
    dot_general x7 -> x5, matrix products: 18.9 us -> 10.6 us  [dot_last(): lax.dot_general(a, b, (((1,), (1,)), ((), ())), preferred_element_type=F32)]
    unnamed x167 -> x109, local copies, waits for them, and re-layouts: 21.1 us -> 13.2 us
    dot_general x7 -> x5, matrix products: 11.9 us -> 4.88 us  [dot(): return jnp.dot(a, b, preferred_element_type=F32)]
  transfers between devices with their start and end apart: 16 -> 16, of which waited for: 3 -> 5; matrix products, arithmetic and copies ran while one was open for 25% -> 16% of each run, Pallas kernels for 66% -> 72%
where the time goes in v2:
time: 535 us; the launch traced here: 532 us
  Pallas kernels  383 us (72%)
  local copies, waits for them, and re-layouts  39.3 us (7%)
  other arithmetic  38.4 us (7%)
  waiting for transfers between devices  26.4 us (5%)
  matrix products  25.4 us (5%)
  starting transfers between devices  17.6 us (3%)
    pallas_call x1, Pallas kernels, experts_fused(): pl.pallas_call(functools.partial(expert_kernel, chips, blks), out_shape=[...  133 us
    pallas_call x3, Pallas kernels, all_gather_blk(): pl.pallas_call(functools.partial(ag_kernel, count, chips, plans), out_sha...  126 us
    pallas_call x2, Pallas kernels, reduce_scatter_blk(): pl.pallas_call(functools.partial(rs_kernel, count, chips, plans), out_sha...  95.4 us
    ppermute x16, waiting for transfers between devices, swap(): return lax.ppermute(array, 'head', [(0, 1), (1, 0)])  26.4 us
    ppermute x16, starting transfers between devices, swap(): return lax.ppermute(array, 'head', [(0, 1), (1, 0)])  17.6 us
    pallas_call x1, Pallas kernels, attention_backward(): pl.pallas_call(functools.partial(backward_kernel, repeats), grid_spec=plt...  17.3 us
    unnamed x109, local copies, waits for them, and re-layouts  13.2 us
    pallas_call x1, Pallas kernels, attention_forward(): pl.pallas_call(functools.partial(forward_kernel, repeats), grid_spec=pltp...  11.6 us
  transfers between devices with their start and end apart: 16, of which 5 were waited for; matrix products, arithmetic and copies ran while one was open for 16% of the time, Pallas kernels for 72%

profile of v2, /device:TPU:0, one launch (start us, length us, event | category | flops | bytes accessed | tf_op | source)
XLA Modules:
  0.0 532.2 jit_solution(16877748066425339172)
XLA Ops:
  5.5 3.0 collective-permute-start.1
  14.8 8.8 %collective-permute-done.2 = bf16[48,1024]{1,0:T(8,128)(2,1)S(1)} collective-permute-done((bf16[48,1024]{1,0:T(8,128)(2,1)S(1)}, bf16[48,1024]{1,0:T(8,128)(2,1)S(1)}, u32[]{:S(2)}, u32[]{:S(2)}) %collective-permute-start.2) | collective-permute-done | bytes 98336 | tf_op jit(solution)/shard_map/ppermute | solution.py:320
  26.3 70.6 %shard_map.258 = (bf16[2,16,48,1024]{3,2,1,0:T(8,128)(2,1)}, bf16[16,48,1536]{2,1,0:T(8,128)(2,1)}, bf16[16,32,1536]{2,1,0:T(8,128)(2,1)}, bf16[16,128,1536]{2,1,0:T(8,128)(2,1)}) custom-call(bf16[2,48,1024]{2,1,0:T(8,128)(2,1)} %maximum_select_fusion.8.refs_0_, bf16[48,1536]{1,0:T(8,128)(2,1)} %refs_1_.1, bf16[32,1536]{1,0:T(8,128)(2,1)} %refs_2_.1, ...), custom_call_target="tpu_custom_call" | custom-call | tf_op jit(solution)/shard_map/pallas_call | solution.py:128
  97.6 28.6 %shard_map.255 = bf16[2,16,48,1408]{3,2,1,0:T(8,128)(2,1)} custom-call(bf16[2,48,1408]{2,1,0:T(8,128)(2,1)} %maximum_select_fusion.7.refs_0_), custom_call_target="tpu_custom_call" | custom-call | tf_op jit(solution)/shard_map/pallas_call | solution.py:128
  126.2 2.3 fusion.50
  133.0 26.8 %shard_map.256 = bf16[16,256,512]{2,1,0:T(8,128)(2,1)} custom-call(bf16[256,512]{1,0:T(8,128)(2,1)} %slice.117.refs_0_), custom_call_target="tpu_custom_call" | custom-call | tf_op jit(solution)/shard_map/pallas_call | solution.py:128
  162.0 11.6 %shard_map.257 = (bf16[256,768]{1,0:T(8,128)(2,1)S(1)}, f32[256,768]{1,0:T(8,128)S(1)}, f32[2,2,384]{2,1,0:T(2,128)S(1)}) custom-call(s32[32]{0:T(128)S(1)} %select_reduce_fusion.slots_ref, s32[2]{0:T(128)S(1)} %dynamic_slice.75.places_ref, s32[3]{0:T(128)S(1)} %bitcast.151, bf16[256,768]{1,0:T(8,128)(2,1)S(1)} %slice.116.q_ref, ...), custom_call_target="tpu_custom_call" | custom-call | tf_op jit(solution)/shard_map/pallas_call | solution.py:389
  175.8 2.4 maximum_select_fusion.4
  178.1 6.2 %collective-permute-done.3 = bf16[128,1536]{1,0:T(8,128)(2,1)} collective-permute-done((bf16[128,1536]{1,0:T(8,128)(2,1)S(1)}, bf16[128,1536]{1,0:T(8,128)(2,1)}, u32[]{:S(2)}, u32[]{:S(2)}) %collective-permute-start.3) | collective-permute-done | bytes 393248 | tf_op jit(solution)/shard_map/ppermute | solution.py:320
  188.9 3.6 maximum_select_fusion.1.out_ref
  204.5 2.7 convolution_convert_fusion.1
  207.2 4.7 maximum_select_fusion
  211.9 132.8 %shard_map.259 = (f32[128,1664]{1,0:T(8,128)}, f32[128,1536]{1,0:T(8,128)}, bf16[1536,1024]{1,0:T(8,128)(2,1)}, bf16[512,1536]{1,0:T(8,128)(2,1)}) custom-call(bf16[128,1664]{1,0:T(8,128)(2,1)} %concatenate.85.ext_ref, bf16[1536,1024]{1,0:T(8,128)(2,1)} %bitcast.155, bf16[512,1536]{1,0:T(8,128)(2,1)} %maximum_select_fusion.1.out_ref, ...), custom_call_target="tpu_custom_call" | custom-call | tf_op jit(solution)/shard_map/pallas_call | solution.py:796
  360.6 4.4 collective-permute-done.10
  366.6 3.5 convolution_convert_fusion.5.grad_ref
  370.1 17.3 %shard_map.260 = (bf16[256,768]{1,0:T(8,128)(2,1)}, bf16[32,128,256]{2,1,0:T(8,128)(2,1)}, bf16[32,128,256]{2,1,0:T(8,128)(2,1)}) custom-call(s32[32]{0:T(128)} %copy-done.4, s32[2]{0:T(128)} %copy-done.5, s32[3]{0:T(128)} %bitcast.152, bf16[256,768]{1,0:T(8,128)(2,1)} %copy-done.1, bf16[32,128,512]{2,1,0:T(8,128)(2,1)} %bitcast.146, ...), custom_call_target="tpu_custom_call" | custom-call | tf_op jit(solution)/shard_map/pallas_call | solution.py:454
  389.2 27.6 %shard_map.261 = (bf16[256,256]{1,0:T(8,128)(2,1)}, bf16[256,256]{1,0:T(8,128)(2,1)}) custom-call(bf16[16,256,256]{2,1,0:T(8,128)(2,1)} %bitcast.180, bf16[16,256,256]{2,1,0:T(8,128)(2,1)} %bitcast.181), custom_call_target="tpu_custom_call" | custom-call | tf_op jit(solution)/shard_map/pallas_call | solution.py:263
  419.9 3.6 fusion
  426.4 3.1 convolution_convert_fusion
  429.5 6.0 %collective-permute-done.11 = bf16[128,1536]{1,0:T(8,128)(2,1)S(1)} collective-permute-done((bf16[128,1536]{1,0:T(8,128)(2,1)S(1)}, bf16[128,1536]{1,0:T(8,128)(2,1)S(1)}, u32[]{:S(2)}, u32[]{:S(2)}) %collective-permute-start.11) | collective-permute-done | bytes 393248 | tf_op jit(solution)/shard_map/ppermute | solution.py:320
  440.0 67.9 %shard_map.262 = (bf16[2,48,1280]{2,1,0:T(8,128)(2,1)}, bf16[2,48,1024]{2,1,0:T(8,128)(2,1)}, f32[48,1536]{1,0:T(8,128)}, f32[32,1536]{1,0:T(8,128)}, f32[2,48,128]{2,1,0:T(8,128)}) custom-call(bf16[2,16,48,1280]{3,2,1,0:T(8,128)(2,1)} %bitcast.153, bf16[2,16,48,1024]{3,2,1,0:T(8,128)(2,1)} %bitcast.154, bf16[16,48,1536]{2,1,0:T(8,128)(2,1)} %bitcast.158, ...), custom_call_target="tpu_custom_call" | custom-call | tf_op jit(solution)/shard_map/pallas_call | solution.py:263
  514.6 2.8 fusion.9
  517.5 2.7 fusion.18
  526.6 3.8 fusion.4
  (226 shorter events, 83.6 us)
Async XLA Ops:
  0.6 13.3 %copy-start.48 = (s32[32]{0:T(128)S(1)}, s32[32]{0:T(128)}, u32[]{:S(2)}) copy-start(s32[32]{0:T(128)} %param.19) | copy-start | bytes 388
  0.7 13.8 %copy-start.49 = (s32[3]{0:T(128)S(1)}, s32[3]{0:T(128)}, u32[]{:S(2)}) copy-start(s32[3]{0:T(128)} %param.18) | copy-start | bytes 40
  5.5 91.3 %collective-permute-start.1 = (bf16[48,1408]{1,0:T(8,128)(2,1)S(1)}, bf16[48,1408]{1,0:T(8,128)(2,1)S(1)}, u32[]{:S(2)}, u32[]{:S(2)}) collective-permute-start(bf16[48,1408]{1,0:T(8,128)(2,1)S(1)} %concatenate.84), channel_id=1, source_target_pairs={{0,16},{16,0},{1,17},{17,1},{2,18},{18,2},{3,19},{19,3},{4,20},{20... | collective-permute-start | bytes 405512 | tf_op jit(solution)/shard_map/ppermute | solution.py:320
  8.6 120.2 %collective-permute-start = (bf16[128,1536]{1,0:T(8,128)(2,1)}, bf16[128,1536]{1,0:T(8,128)(2,1)S(1)}, u32[]{:S(2)}, u32[]{:S(2)}) collective-permute-start(bf16[128,1536]{1,0:T(8,128)(2,1)} %param.16), channel_id=1, source_target_pairs={{0,16},{16,0},{1,17},{17,1},{2,18},{18,2},{3,19},{19,3},{4,20},{20... | collective-permute-start | bytes 1179656 | tf_op jit(solution)/shard_map/ppermute | solution.py:320
  9.9 13.6 %collective-permute-start.2 = (bf16[48,1024]{1,0:T(8,128)(2,1)S(1)}, bf16[48,1024]{1,0:T(8,128)(2,1)S(1)}, u32[]{:S(2)}, u32[]{:S(2)}) collective-permute-start(bf16[48,1024]{1,0:T(8,128)(2,1)S(1)} %bitcast.195), channel_id=1, source_target_pairs={{0,16},{16,0},{1,17},{17,1},{2,18},{18,2},{3,19},{19,3},{4,20},{20... | collective-permute-start | bytes 294920 | tf_op jit(solution)/shard_map/ppermute | solution.py:320
  11.9 177.0 %collective-permute-start.5 = (bf16[512,768]{1,0:T(8,128)(2,1)}, bf16[512,768]{1,0:T(8,128)(2,1)}, u32[]{:S(2)}, u32[]{:S(2)}) collective-permute-start(bf16[512,768]{1,0:T(8,128)(2,1)} %bitcast.22), channel_id=1, source_target_pairs={{0,16},{16,0},{1,17},{17,1},{2,18},{18,2},{3,19},{19,3},{4,20},{20... | collective-permute-start | bytes 2359304 | tf_op jit(solution)/shard_map/ppermute | solution.py:320
  12.0 195.2 %collective-permute-start.4 = (bf16[768,1024]{1,0:T(8,128)(2,1)}, bf16[768,1024]{1,0:T(8,128)(2,1)}, u32[]{:S(2)}, u32[]{:S(2)}) collective-permute-start(bf16[768,1024]{1,0:T(8,128)(2,1)} %bitcast.19), channel_id=1, source_target_pairs={{0,16},{16,0},{1,17},{17,1},{2,18},{18,2},{3,19},{19,3},{4,20},{20... | collective-permute-start | bytes 4718600 | tf_op jit(solution)/shard_map/ppermute | solution.py:320
  14.3 145.5 %copy-start.4 = (s32[32]{0:T(128)}, s32[32]{0:T(128)S(1)}, u32[]{:S(2)}) copy-start(s32[32]{0:T(128)S(1)} %select_reduce_fusion.slots_ref) | copy-start | bytes 388
  14.4 145.4 %copy-start.5 = (s32[2]{0:T(128)}, s32[2]{0:T(128)S(1)}, u32[]{:S(2)}) copy-start(s32[2]{0:T(128)S(1)} %dynamic_slice.75.places_ref) | copy-start | bytes 28
  14.6 145.2 %copy-start.6 = (s32[3,1]{0,1:T(1,128)}, s32[3,1]{0,1:T(1,128)S(1)}, u32[]{:S(2)}) copy-start(s32[3,1]{0,1:T(1,128)S(1)} %reduce-window.9) | copy-start | bytes 40
  23.5 152.3 %collective-permute-start.8 = (bf16[128,1536]{1,0:T(8,128)(2,1)}, bf16[128,1536]{1,0:T(8,128)(2,1)}, u32[]{:S(2)}, u32[]{:S(2)}) collective-permute-start(bf16[128,1536]{1,0:T(8,128)(2,1)} %refs_3_.1), channel_id=1, source_target_pairs={{0,16},{16,0},{1,17},{17,1},{2,18},{18,2},{3,19},{19,3},{4,20},{20... | collective-permute-start | bytes 1179656 | tf_op jit(solution)/shard_map/ppermute | solution.py:320
  132.9 26.9 %copy-start.1 = (bf16[256,768]{1,0:T(8,128)(2,1)}, bf16[256,768]{1,0:T(8,128)(2,1)S(1)}, u32[]{:S(2)}) copy-start(bf16[256,768]{1,0:T(8,128)(2,1)S(1)} %slice.116.q_ref) | copy-start | bytes 1179652
  174.6 9.7 %collective-permute-start.3 = (bf16[128,1536]{1,0:T(8,128)(2,1)S(1)}, bf16[128,1536]{1,0:T(8,128)(2,1)}, u32[]{:S(2)}, u32[]{:S(2)}) collective-permute-start(bf16[128,1536]{1,0:T(8,128)(2,1)S(1)} %fusion.36), channel_id=1, source_target_pairs={{0,16},{16,0},{1,17},{17,1},{2,18},{18,2},{3,19},{19,3},{4,20},{20... | collective-permute-start | bytes 1179656 | tf_op jit(solution)/shard_map/ppermute | solution.py:320
  185.6 165.0 %copy-start.41 = (f32[128]{0:T(128)}, f32[128]{0:T(128)S(1)}, u32[]{:S(2)}) copy-start(f32[128]{0:T(128)S(1)} %add_rsqrt_fusion.1) | copy-start | bytes 1540
  185.8 7.8 %collective-permute-start.6 = (bf16[128,1536]{1,0:T(8,128)(2,1)S(1)}, bf16[128,1536]{1,0:T(8,128)(2,1)S(1)}, u32[]{:S(2)}, u32[]{:S(2)}) collective-permute-start(bf16[128,1536]{1,0:T(8,128)(2,1)S(1)} %multiply_convert_fusion), channel_id=1, source_target_pairs={{0,16},{16,0},{1,17},{17,1},{2,18},{18,2},{3,19},{19,3},{4,20},{20... | collective-permute-start | bytes 1179656 | tf_op jit(solution)/shard_map/ppermute | solution.py:320
  188.9 246.6 %copy-start.44 = (f32[128]{0:T(128)}, f32[128]{0:T(128)S(1)}, u32[]{:S(2)}) copy-start(f32[128]{0:T(128)S(1)} %add_rsqrt_fusion) | copy-start | bytes 1540
  198.1 150.4 %collective-permute-start.9 = (bf16[128,1536]{1,0:T(8,128)(2,1)}, bf16[128,1536]{1,0:T(8,128)(2,1)}, u32[]{:S(2)}, u32[]{:S(2)}) collective-permute-start(bf16[128,1536]{1,0:T(8,128)(2,1)} %fusion.38), channel_id=1, source_target_pairs={{0,16},{16,0},{1,17},{17,1},{2,18},{18,2},{3,19},{19,3},{4,20},{20... | collective-permute-start | bytes 1179656 | tf_op jit(solution)/shard_map/ppermute | solution.py:320
  201.3 316.1 %collective-permute-start.7 = (bf16[128,1536]{1,0:T(8,128)(2,1)}, bf16[128,1536]{1,0:T(8,128)(2,1)}, u32[]{:S(2)}, u32[]{:S(2)}) collective-permute-start(bf16[128,1536]{1,0:T(8,128)(2,1)} %fusion.37), channel_id=1, source_target_pairs={{0,16},{16,0},{1,17},{17,1},{2,18},{18,2},{3,19},{19,3},{4,20},{20... | collective-permute-start | bytes 1179656 | tf_op jit(solution)/shard_map/ppermute | solution.py:320
  353.0 12.0 %collective-permute-start.10 = (bf16[128,1536]{1,0:T(8,128)(2,1)}, bf16[128,1536]{1,0:T(8,128)(2,1)}, u32[]{:S(2)}, u32[]{:S(2)}) collective-permute-start(bf16[128,1536]{1,0:T(8,128)(2,1)} %fusion.49), channel_id=1, source_target_pairs={{0,16},{16,0},{1,17},{17,1},{2,18},{18,2},{3,19},{19,3},{4,20},{20... | collective-permute-start | bytes 1179656 | tf_op jit(solution)/shard_map/ppermute | solution.py:320
  354.7 159.9 %collective-permute-start.15 = (bf16[512,768]{1,0:T(8,128)(2,1)}, bf16[512,768]{1,0:T(8,128)(2,1)}, u32[]{:S(2)}, u32[]{:S(2)}) collective-permute-start(bf16[512,768]{1,0:T(8,128)(2,1)} %fusion.22), channel_id=1, source_target_pairs={{0,16},{16,0},{1,17},{17,1},{2,18},{18,2},{3,19},{19,3},{4,20},{20... | collective-permute-start | bytes 2359304 | tf_op jit(solution)/shard_map/ppermute | solution.py:320
  357.4 169.1 %collective-permute-start.14 = (bf16[768,1024]{1,0:T(8,128)(2,1)}, bf16[768,1024]{1,0:T(8,128)(2,1)}, u32[]{:S(2)}, u32[]{:S(2)}) collective-permute-start(bf16[768,1024]{1,0:T(8,128)(2,1)} %dynamic-slice_bitcast_fusion), channel_id=1, source_target_pairs={{0,16},{16,0},{1,17},{17,1},{2,18},{18,2},{3,19},{19,3},{4,20},{20... | collective-permute-start | bytes 4718600 | tf_op jit(solution)/shard_map/ppermute | solution.py:320
  423.6 11.9 %collective-permute-start.11 = (bf16[128,1536]{1,0:T(8,128)(2,1)S(1)}, bf16[128,1536]{1,0:T(8,128)(2,1)S(1)}, u32[]{:S(2)}, u32[]{:S(2)}) collective-permute-start(bf16[128,1536]{1,0:T(8,128)(2,1)S(1)} %fusion.39), channel_id=1, source_target_pairs={{0,16},{16,0},{1,17},{17,1},{2,18},{18,2},{3,19},{19,3},{4,20},{20... | collective-permute-start | bytes 1179656 | tf_op jit(solution)/shard_map/ppermute | solution.py:320
  510.5 11.1 %collective-permute-start.13 = (bf16[48,2304]{1,0:T(8,128)(2,1)}, bf16[48,2304]{1,0:T(8,128)(2,1)}, u32[]{:S(2)}, u32[]{:S(2)}) collective-permute-start(bf16[48,2304]{1,0:T(8,128)(2,1)} %pad_maximum_fusion.1), channel_id=1, source_target_pairs={{0,16},{16,0},{1,17},{17,1},{2,18},{18,2},{3,19},{19,3},{4,20},{20... | collective-permute-start | bytes 663560 | tf_op jit(solution)/shard_map/ppermute | solution.py:320
  511.8 8.5 %collective-permute-start.12 = (f32[48,128]{1,0:T(8,128)S(1)}, f32[48,128]{1,0:T(8,128)S(1)}, u32[]{:S(2)}, u32[]{:S(2)}) collective-permute-start(f32[48,128]{1,0:T(8,128)S(1)} %dynamic-slice_bitcast_fusion.5), channel_id=1, source_target_pairs={{0,16},{16,0},{1,17},{17,1},{2,18},{18,2},{3,19},{19,3},{4,20},{20... | collective-permute-start | bytes 73736 | tf_op jit(solution)/shard_map/ppermute | solution.py:320
  (42 other events, 148.4 us)
